TPU v7x, 128 devices: a whole 4x4x4 slice. The times are simulated.
128 devices in a mesh: group: 16 (over z, y), tp: 8 (over x, core).
Axes of the slice: x: 4, y: 4, z: 4, core: 2. Of those that a mesh axis runs over, the one named last changes fastest.
Arguments:
- fresh: bfloat16 [1536, 8, 64, 256], P(('group', 'tp')), may hold values from -18 to 18
- lengths: int32 [256], P('group'), may hold values from 1 to 508, as said below
- owner_table: int32 [256, 8], P('group'), may hold values from 0 to 95, as said below
- decode_slot: int32 [256], P('group'), may hold values from 0 to 255, as said below
- decode_table: int32 [256, 8], P('group'), may hold values from 0 to 127, as said below
- queries: bfloat16 [256, 4, 8192], P('group', None, 'tp'), may hold values from -24 to 24
- new_kv: bfloat16 [256, 4, 2048], P('group', None, 'tp'), may hold values from -6 to 6
Outputs:
- page_pool: bfloat16 [2048, 8, 64, 256], P('group', 'tp')
- attended: bfloat16 [256, 4, 8192], P('group', None, 'tp')
Inputs may be any that keep to these rules, and one draw needn't show every extreme that they name: Each request has 1 to 8 pages, ceil(lengths[r] / 64); the pages of one group's requests add up to exactly 96; the pages of one home group's requests that are decoded on one group add up to at most 14, exactly 14 for some group; lengths[r] + 4 <= 512. `owner_table`: for j < ceil(lengths[r] / 64) the entries name distinct fresh pages across all requests of one home group; later entries are unused. `decode_slot`: A permutation of all slots, so each group decodes exactly 16 requests. Of one home group's requests, 0, 1 or 2 are decoded on any one group, and 2 on some group. `decode_table`: the 16 rows of one group hold each of its 128 pool pages exactly once.
All inputs are finite; a program needn't handle non-finite values.
Results may differ from a plain program's by a relative error of at most 0.012.
Values may be sent and summed in bfloat16 or wider, within the bound.
No kernel may reach another device: no remote copies, remote signals or barrier semaphores. Data moves between devices by JAX's collectives and lax.ppermute only.
A program may use at most 128 MiB of HBM per device.

v0:
```python
import jax
import jax.numpy as jnp
from jax import lax
from jax.sharding import PartitionSpec as P

HEADS = 64
KVH = 8


def first_index(matches):
    columns = jnp.arange(matches.shape[1], dtype=jnp.int32)
    return jnp.sum(jnp.where(matches, columns[None, :], 0), axis=1)


def token_mask(tile_set, lengths_in, page_len):
    maxpages = tile_set.shape[1]
    position = jnp.arange(maxpages)[:, None] * page_len + jnp.arange(page_len)[None, :]
    inside = position[None, :, :] < lengths_in[:, None, None]
    return jnp.where(inside[:, :, None, :, None], tile_set, jnp.zeros((), tile_set.dtype))


def page_tiles(page_store, table_rows, lengths_in, page_len):
    shaped = (table_rows.shape[0], table_rows.shape[1]) + page_store.shape[1:]
    picked = jnp.take(page_store, table_rows.reshape(-1), axis=0).reshape(shaped)
    return token_mask(picked, lengths_in, page_len)


def append_tokens(tile_set, new_rows, lengths_in, page_len):
    row_count = new_rows.shape[0]
    step_count = new_rows.shape[1]
    tokens = new_rows.reshape(row_count, step_count, tile_set.shape[2], tile_set.shape[4])
    target = lengths_in[:, None] + jnp.arange(step_count, dtype=jnp.int32)[None, :]
    row_index = jnp.arange(row_count, dtype=jnp.int32)[:, None]
    return tile_set.at[row_index, target // page_len, :, target % page_len, :].set(tokens)


def attend(query_rows, tile_set, lengths_in, group_heads):
    row_count, step_count, row_width = query_rows.shape
    maxpages, kv_heads, page_len, doubled = tile_set.shape[1:]
    head_dim = doubled // 2
    shaped = query_rows.reshape(row_count, step_count, kv_heads, group_heads, head_dim)
    key_part = tile_set[..., :head_dim]
    value_part = tile_set[..., head_dim:]
    scores = jnp.einsum("rskgd,rjkpd->rkgsjp", shaped, key_part, preferred_element_type=jnp.float32)
    scores = scores * head_dim ** (-0.5)
    position = jnp.arange(maxpages)[:, None] * page_len + jnp.arange(page_len)[None, :]
    horizon = lengths_in[:, None] + jnp.arange(step_count)[None, :] + 1
    inside = position[None, None, :, :] < horizon[:, :, None, None]
    scores = jnp.where(inside[:, None, None], scores, -jnp.inf)
    highest = jnp.max(scores, axis=(4, 5), keepdims=True)
    weights = jnp.exp(scores - highest)
    totals = jnp.sum(weights, axis=(4, 5), keepdims=True)
    soft_weights = (weights / totals).astype(jnp.bfloat16)
    mixture = jnp.einsum(
        "rkgsjp,rjkpd->rskgd", soft_weights, value_part, preferred_element_type=jnp.float32
    )
    return mixture.astype(jnp.bfloat16).reshape(row_count, step_count, row_width)


def shards(fresh, lengths, owner_table, decode_slot, decode_table, queries, new_kv):
    groups = lax.axis_size("group")
    local_reqs = lengths.shape[0]
    maxpages = owner_table.shape[1]
    page_len = fresh.shape[2]
    capacity = 2 * local_reqs // groups
    entries = groups * capacity
    group_heads = HEADS // KVH
    head_pages = lax.all_to_all(fresh, "tp", split_axis=1, concat_axis=0, tiled=True)
    destination = decode_slot // local_reqs
    onehot = (destination[:, None] == jnp.arange(groups, dtype=jnp.int32)[None, :]).astype(
        jnp.int32
    )
    position = jnp.sum((jnp.cumsum(onehot, axis=0) - onehot) * onehot, axis=1)
    bucket = destination * capacity + position
    in_bucket = bucket[None, :] == jnp.arange(entries, dtype=jnp.int32)[:, None]
    filled = jnp.any(in_bucket, axis=1)
    chosen = first_index(in_bucket)
    send_len = jnp.sum(jnp.where(in_bucket, lengths[None, :], 0), axis=1)
    slot_within = jnp.sum(jnp.where(in_bucket, (decode_slot % local_reqs)[None, :], 0), axis=1)
    send_slot = jnp.where(filled, slot_within, -1)
    packed = page_tiles(head_pages, jnp.take(owner_table, chosen, axis=0), send_len, page_len)
    labels = jnp.stack([send_slot, send_len], axis=1)
    arrived, arrived_labels = (
        lax.all_to_all(packed, "group", split_axis=0, concat_axis=0, tiled=True),
        lax.all_to_all(labels, "group", split_axis=0, concat_axis=0, tiled=True),
    )
    slot_match = arrived_labels[:, 0][None, :] == jnp.arange(local_reqs, dtype=jnp.int32)[:, None]
    slot_len = jnp.sum(jnp.where(slot_match, arrived_labels[:, 1][None, :], 0), axis=1).astype(
        jnp.int32
    )
    slot_tiles = jnp.take(arrived, first_index(slot_match), axis=0)
    slot_tiles = append_tokens(slot_tiles, new_kv, slot_len, page_len)
    flat_shape = (local_reqs * maxpages,) + slot_tiles.shape[2:]
    page_pool = (
        jnp.zeros(flat_shape, slot_tiles.dtype)
        .at[decode_table.reshape(-1)]
        .set(slot_tiles.reshape(flat_shape))
    )
    attended = attend(queries, slot_tiles, slot_len, group_heads)
    return (page_pool, attended)


def solution(mesh):
    return jax.shard_map(
        shards,
        mesh=mesh,
        in_specs=(
            P(("group", "tp"), None, None, None),
            P("group"),
            P("group", None),
            P("group"),
            P("group", None),
            P("group", None, "tp"),
            P("group", None, "tp"),
        ),
        out_specs=(P("group", "tp", None, None), P("group", None, "tp")),
        check_vma=False,
    )
```

profile of v0, /device:TPU:0, one launch (start us, length us, event | category | flops | bytes accessed | tf_op | source)
XLA Modules:
  0.0 248.5 jit_solution(5121142640256613193)
XLA Ops:
  0.6 4.0 %copy.29 = bf16[12,8,64,256]{3,2,0,1:T(8,128)(2,1)} copy(bf16[12,8,64,256]{3,2,1,0:T(8,128)(2,1)} %param.7) | data formatting | bytes 6291456 | tf_op args[0]
  4.6 0.0 copy-start.6
  4.6 4.5 %all-to-all-start.1 = ((bf16[12,8,64,256]{3,2,0,1:T(8,128)(2,1)}), bf16[12,8,64,256]{3,2,0,1:T(8,128)(2,1)S(1)}, u32[]{:S(2)}, u32[]{:S(2)}) async-start(bf16[12,8,64,256]{3,2,0,1:T(8,128)(2,1)} %copy.29), calls=%async_computation.1 | async-start | bytes 6291456 | tf_op jit(solution)/shard_map/all_to_all | solution.py:68
  9.1 0.0 copy-done.6
  9.1 0.1 fusion.18
  9.3 0.2 select_reduce_fusion.5
  9.4 0.1 fusion.17
  9.5 0.0 copy-done.5
  9.5 0.1 select_reduce_fusion.4
  9.7 0.1 select_n.213
  9.7 0.1 stack.7
  9.8 0.6 copy.26
  10.5 0.0 copy-done.3
  10.5 0.1 copy.28
  10.5 0.6 gather_fusion
  11.1 0.1 compare_and_fusion
  11.2 0.1 select_n.222
  11.3 0.1 iota_add_fusion.1
  11.4 0.1 broadcast_compare_fusion.1
  11.5 36.0 %all-to-all-done.1 = bf16[12,8,64,256]{3,2,0,1:T(8,128)(2,1)S(1)} async-done(((bf16[12,8,64,256]{3,2,0,1:T(8,128)(2,1)}), bf16[12,8,64,256]{3,2,0,1:T(8,128)(2,1)S(1)}, u32[]{:S(2)}, u32[]{:S(2)}) %all-to-all-start.1) | async-done | bytes 3145760 | tf_op jit(solution)/shard_map/all_to_all | solution.py:68
  47.6 8.0 %all-to-all-start = ((s32[16,2,2]{1,2,0:T(2,128)}), s32[16,2,2]{1,2,0:T(2,128)S(1)}, u32[]{:S(2)}, u32[]{:S(2)}) async-start(s32[16,2,2]{1,2,0:T(2,128)} %copy.26), calls=%async_computation | async-start | bytes 32768 | tf_op jit(solution)/shard_map/all_to_all | solution.py:85
  55.6 8.5 %gather_fusion.1 = bf16[256,64,256]{2,1,0:T(8,128)(2,1)} fusion(bf16[96,64,256]{2,1,0:T(8,128)(2,1)S(1)} %bitcast.90, s32[1024]{0:T(1024)S(1)} %pad_clamp_fusion.1), kind=kCustom, calls=%fused_computation.1 | custom fusion | bytes 16778240 | tf_op jit(solution)/shard_map/jit(_take)/gather | solution.py:24
  64.1 8.1 %select_select_fusion = bf16[32,8,1,64,256]{4,3,1,2,0:T(8,128)(2,1)} fusion(bf16[32,8,1,64,256]{4,3,1,2,0:T(8,128)(2,1)} %bitcast.91, pred[32,8]{1,0:T(8,128)(4,1)S(1)} %get-tuple-element.7, pred[32,8,64]{2,1,0:T(8,128)(4,1)S(1)} %broadcast_compare_fusion.1), kind=kLoop, calls=%fused_computation.5 | loop fusion | flops 8388608 | bytes 16793856 | tf_op jit(solution)/shard_map/jit(_where)/select_n | solution.py:19
  72.2 0.0 all-to-all-done
  72.2 7.4 %all-to-all-start.2 = ((bf16[32,8,1,64,256]{4,3,1,2,0:T(8,128)(2,1)}), bf16[32,8,1,64,256]{4,3,1,2,0:T(8,128)(2,1)}, u32[]{:S(2)}, u32[]{:S(2)}) async-start(bf16[32,8,1,64,256]{4,3,1,2,0:T(8,128)(2,1)} %select_select_fusion), calls=%async_computation.2 | async-start | bytes 16777216 | tf_op jit(solution)/shard_map/all_to_all | solution.py:84
  79.6 0.0 copy-done.2
  79.7 0.0 copy-done.1
  79.7 0.1 reshape.479
  79.7 0.0 copy-done.4
  79.8 0.1 copy.25
  79.8 0.1 reshape.416
  79.9 0.1 all_to_all.23
  80.0 0.1 select_reduce_fusion
  80.1 0.1 fusion.13
  80.2 0.1 reshape.456
  80.4 0.1 add_add_fusion
  80.4 0.1 broadcast_compare_fusion
  80.6 121.3 %all-to-all-done.2 = bf16[32,8,1,64,256]{4,3,1,2,0:T(8,128)(2,1)} async-done(((bf16[32,8,1,64,256]{4,3,1,2,0:T(8,128)(2,1)}), bf16[32,8,1,64,256]{4,3,1,2,0:T(8,128)(2,1)}, u32[]{:S(2)}, u32[]{:S(2)}) %all-to-all-start.2) | async-done | bytes 8388640 | tf_op jit(solution)/shard_map/all_to_all | solution.py:84
  201.9 6.2 %gather_fusion.2 = bf16[16,8,64,256]{3,2,1,0:T(8,128)(2,1)} fusion(bf16[32,8,64,256]{3,2,1,0:T(8,128)(2,1)} %bitcast.10, s32[1024]{0:T(1024)S(1)} %pad_clamp_fusion), kind=kCustom, calls=%fused_computation.2 | custom fusion | bytes 8388672 | tf_op jit(solution)/shard_map/jit(_take)/gather | solution.py:91
  208.1 4.6 %fusion = bf16[16,8,64,256]{3,2,1,0:T(8,128)(2,1)} fusion(bf16[16,8,64,256]{3,2,1,0:T(8,128)(2,1)} %gather_fusion.2, pred[16]{0:T(512)(128)(4,1)S(1)} %compare_and_fusion.2), kind=kLoop, calls=%fused_computation.7 | loop fusion | flops 2097152 | bytes 8388624 | tf_op jit(solution)/shard_map/jit(_take)/select_n | solution.py:91
  212.7 8.1 %scatter_fusion = bf16[16,8,64,256]{3,2,1,0:T(8,128)(2,1)} fusion(bf16[16,8,64,256]{3,2,1,0:T(8,128)(2,1)} %fusion, s32[64]{0:T(128)S(1)} %reshape.456, bf16[64,256]{1,0:T(8,128)(2,1)S(1)} %reshape.458), kind=kCustom, calls=%fused_computation.3 | custom fusion | bytes 99072 | tf_op jit(solution)/shard_map/scatter | solution.py:34
  220.8 3.9 %fusion.26 = (f32[16,8,4]{1,2,0:T(4,128)S(1)}, f32[16,1,8,4,8,64]{5,2,3,4,0,1:T(8,128)S(1)}) fusion(bf16[16,4,8,128,1]{3,2,1,0,4:T(8,128)(2,1)S(1)} %reshape.479, bf16[16,8,1,64,256]{4,3,1,0,2:T(8,128)(2,1)} %bitcast.92, pred[16,4,8,64]{3,1,2,0:T(4,128)(4,1)S(1)} %broadcast_compare_fusion), kind=kOutput, calls=%fused_computation.91 | convolution fusion | flops 67894784 | bytes 3311616 | tf_op jit(solution)/shard_map/rskgd,rjkpd->rkgsjp/dot_general | solution.py:44
  224.7 0.5 fusion.3
  225.2 0.0 copy-done
  225.2 0.7 fusion.6
  226.0 0.7 reshape.423
  226.7 2.5 %broadcast.467 = bf16[128,64,256]{2,1,0:T(8,128)(2,1)} broadcast(bf16[]{:T(256)} %constant.103.clone.1), dimensions={} | broadcast | bytes 4194306 | tf_op jit(solution)/shard_map/broadcast_in_dim | solution.py:95
  229.2 19.3 %scatter_fusion.1 = bf16[128,64,256]{2,1,0:T(8,128)(2,1)} fusion(bf16[128,64,256]{2,1,0:T(8,128)(2,1)} %broadcast.467, s32[128]{0:T(128)S(1)} %fusion.23, bf16[128,64,256]{2,1,0:T(8,128)(2,1)} %bitcast.93), kind=kCustom, calls=%fused_computation.4 | custom fusion | bytes 12583424 | tf_op jit(solution)/shard_map/scatter | solution.py:97
  (24 shorter events, 0.2 us)
Async XLA Ops:
  4.6 4.5 %copy-start.6 = (s32[16]{0:T(128)S(1)}, s32[16]{0:T(128)}, u32[]{:S(2)}) copy-start(s32[16]{0:T(128)} %param.10) | copy-start | bytes 196
  4.6 4.9 %copy-start.5 = (s32[16]{0:T(128)S(1)}, s32[16]{0:T(128)}, u32[]{:S(2)}) copy-start(s32[16]{0:T(128)} %param.8) | copy-start | bytes 196
  4.6 5.9 %copy-start.3 = (s32[16,8]{0,1:T(8,128)S(1)}, s32[16,8]{0,1:T(8,128)}, u32[]{:S(2)}) copy-start(s32[16,8]{0,1:T(8,128)} %param.9) | copy-start | bytes 1540
  4.6 43.0 %all-to-all-start.1 = ((bf16[12,8,64,256]{3,2,0,1:T(8,128)(2,1)}), bf16[12,8,64,256]{3,2,0,1:T(8,128)(2,1)S(1)}, u32[]{:S(2)}, u32[]{:S(2)}) async-start(bf16[12,8,64,256]{3,2,0,1:T(8,128)(2,1)} %copy.29), calls=%async_computation.1 | async-start | bytes 6291456 | tf_op jit(solution)/shard_map/all_to_all | solution.py:68
  47.6 24.7 %all-to-all-start = ((s32[16,2,2]{1,2,0:T(2,128)}), s32[16,2,2]{1,2,0:T(2,128)S(1)}, u32[]{:S(2)}, u32[]{:S(2)}) async-start(s32[16,2,2]{1,2,0:T(2,128)} %copy.26), calls=%async_computation | async-start | bytes 32768 | tf_op jit(solution)/shard_map/all_to_all | solution.py:85
  72.2 7.4 %copy-start.2 = (bf16[16,4,256]{2,1,0:T(4,128)(2,1)S(1)}, bf16[16,4,256]{2,1,0:T(4,128)(2,1)}, u32[]{:S(2)}) copy-start(bf16[16,4,256]{2,1,0:T(4,128)(2,1)} %param.13) | copy-start | bytes 98308
  72.2 7.4 %copy-start.1 = (bf16[16,4,1024]{2,1,0:T(4,128)(2,1)S(1)}, bf16[16,4,1024]{2,1,0:T(4,128)(2,1)}, u32[]{:S(2)}) copy-start(bf16[16,4,1024]{2,1,0:T(4,128)(2,1)} %param.12) | copy-start | bytes 393220
  72.2 7.5 %copy-start.4 = (s32[16,8]{0,1:T(8,128)S(1)}, s32[16,8]{0,1:T(8,128)}, u32[]{:S(2)}) copy-start(s32[16,8]{0,1:T(8,128)} %param.11) | copy-start | bytes 1540
  72.2 129.7 %all-to-all-start.2 = ((bf16[32,8,1,64,256]{4,3,1,2,0:T(8,128)(2,1)}), bf16[32,8,1,64,256]{4,3,1,2,0:T(8,128)(2,1)}, u32[]{:S(2)}, u32[]{:S(2)}) async-start(bf16[32,8,1,64,256]{4,3,1,2,0:T(8,128)(2,1)} %select_select_fusion), calls=%async_computation.2 | async-start | bytes 16777216 | tf_op jit(solution)/shard_map/all_to_all | solution.py:84
  220.8 4.4 %copy-start = (bf16[16,8,64,256]{3,2,1,0:T(8,128)(2,1)S(1)}, bf16[16,8,64,256]{3,2,1,0:T(8,128)(2,1)}, u32[]{:S(2)}) copy-start(bf16[16,8,64,256]{3,2,1,0:T(8,128)(2,1)} %scatter_fusion) | copy-start | bytes 12582916
where the time goes:
time: 249 us; the launch traced here: 248 us
  waiting for transfers between devices  157 us (63%)
  local copies, waits for them, and re-layouts  51.2 us (21%)
  starting transfers between devices  19.9 us (8%)
  other arithmetic  14.5 us (6%)
  matrix products  4.6 us (2%)
    all_to_all x1, waiting for transfers between devices, shards(): lax.all_to_all(packed, 'group', split_axis=0, concat_axis=0, tiled=True)  121 us
    all_to_all x1, waiting for transfers between devices, shards(): lax.all_to_all(fresh, 'tp', split_axis=1, concat_axis=0, tiled=True)  36 us
    scatter x1, local copies, waits for them, and re-layouts, shards(): page_pool = jnp.zeros(flat_shape, slot_tiles.dtype).at[decode_table.resha...  19.3 us
    gather x1, local copies, waits for them, and re-layouts, page_tiles(): jnp.take(page_store, table_rows.reshape(-1), axis=0).reshape(shaped)  8.51 us
    select_n x1, other arithmetic, token_mask(): jnp.where(inside[:, :, None, :, None], tile_set, jnp.zeros((), tile_set.d...  8.1 us
    scatter x1, local copies, waits for them, and re-layouts, append_tokens(): tile_set.at[row_index, target // page_len, :, target % page_len, :]  8.1 us
    all_to_all x1, starting transfers between devices, shards(): lax.all_to_all(labels, 'group', split_axis=0, concat_axis=0, tiled=True)  8.05 us
    all_to_all x1, starting transfers between devices, shards(): lax.all_to_all(packed, 'group', split_axis=0, concat_axis=0, tiled=True)  7.38 us
  transfers between devices with their start and end apart: 3, of which 2 were waited for; matrix products, arithmetic and copies ran while one was open for 8% of the time, Pallas kernels for 0%

commit v1 on v0

v1 whole, which is shorter than its diff:
```python
import functools

import jax
import jax.numpy as jnp
from jax import lax
from jax.experimental import pallas as pl
from jax.experimental.pallas import tpu as pltpu
from jax.sharding import PartitionSpec as P

HEADS = 64
KVH = 8
HD = 128
PAGE = 64
STEPS = 4
MAXP = 8
REQ_G = 16
GROUPS = 16
TP = 8
PAGES_D = 12
ROWS = 8
ROW_TILES = PAGE // ROWS
TILES = PAGES_D + 1
ENTRIES = REQ_G * MAXP
GH = HEADS // KVH


def cut_kernel(fresh_ref, meta_ref, out_ref):
    for half in range(2):
        for head in range(KVH):
            row = half * KVH + head
            for page in range(PAGES_D):
                out_ref[row, page] = fresh_ref[page, head, 0, :, half * HD:(half + 1) * HD]
            out_ref[row, PAGES_D] = meta_ref[...]


def cut(fresh, meta):
    return pl.pallas_call(
        cut_kernel,
        grid=(ROW_TILES,),
        in_specs=[
            pl.BlockSpec((PAGES_D, KVH, 1, ROWS, 2 * HD), lambda i: (0, 0, i, 0, 0)),
            pl.BlockSpec((ROWS, HD), lambda i: (0, 0)),
        ],
        out_specs=pl.BlockSpec((2 * KVH, TILES, ROWS, HD), lambda i: (i, 0, 0, 0)),
        out_shape=jax.ShapeDtypeStruct((GROUPS * TP, TILES, ROWS, HD), jnp.bfloat16),
        name="cut",
    )(fresh, meta)


def pick_kernel(got_ref, out_ref, len_ref, ints, table, sem):
    for home in range(GROUPS):
        tile = got_ref[home * TP * TILES + PAGES_D]
        ints[pl.ds(home * ROWS, ROWS), :] = tile.astype(jnp.float32).astype(jnp.int32)
    copy = pltpu.make_async_copy(ints, table, sem)
    copy.start()
    copy.wait()

    def one_home(home, carry):
        row = home * ROWS
        base = home * (TP * TILES)
        for item in range(REQ_G):
            slot = table[row + 2, REQ_G + item] * REQ_G + table[row + 3, REQ_G + item]
            len_ref[slot] = table[row + 1, REQ_G + item] * PAGE + table[row, REQ_G + item]
            for j in range(MAXP):
                out_ref[slot * MAXP + j] = got_ref[base + table[row + j, item]]
        return carry

    lax.fori_loop(0, GROUPS, one_home, 0)


def pick(got):
    return pl.pallas_call(
        pick_kernel,
        in_specs=[pl.BlockSpec(memory_space=pltpu.VMEM)],
        out_specs=[
            pl.BlockSpec(memory_space=pltpu.VMEM),
            pl.BlockSpec(memory_space=pltpu.SMEM),
        ],
        out_shape=[
            jax.ShapeDtypeStruct((GROUPS * ENTRIES, ROWS, HD), jnp.bfloat16),
            jax.ShapeDtypeStruct((GROUPS * REQ_G,), jnp.int32),
        ],
        scratch_shapes=[
            pltpu.VMEM((GROUPS * ROWS, HD), jnp.int32),
            pltpu.SMEM((GROUPS * ROWS, HD), jnp.int32),
            pltpu.SemaphoreType.DMA,
        ],
        compiler_params=pltpu.CompilerParams(vmem_limit_bytes=40 * 1024 * 1024),
        name="pick",
    )(got)


def serve_kernel(len_ref, table_ref, arrived_ref, query_ref, new_ref, pool_ref, out_ref, tiles, sems):
    slot = pl.program_id(0)
    buf = lax.rem(slot, 2)
    length = len_ref[slot]

    def page_copy(which, j):
        at = lax.rem(which, 2)
        return pltpu.make_async_copy(
            tiles.at[at, j], pool_ref.at[table_ref[which * MAXP + j]], sems.at[at, j]
        )

    @pl.when(slot >= 2)
    def _():
        for j in range(MAXP):
            page_copy(slot - 2, j).wait()

    row = lax.broadcasted_iota(jnp.int32, (ROWS, HD), 0)
    fresh_rows = new_ref[0].astype(jnp.float32)
    for j in range(MAXP):
        for rt in range(ROW_TILES):
            at = row + (j * PAGE + rt * ROWS) - length
            for half in range(2):
                lanes = slice(half * HD, (half + 1) * HD)
                x = arrived_ref[2 * rt + half, 0, j].astype(jnp.float32)
                x = jnp.where(at < 0, x, 0.0)
                for u in range(STEPS):
                    x = jnp.where(at == u, fresh_rows[u:u + 1, lanes], x)
                tiles[buf, j, rt, :, lanes] = x.astype(jnp.bfloat16)
    for j in range(MAXP):
        page_copy(slot, j).start()

    span = MAXP * PAGE
    key = tiles[buf, :, :, :, :HD].reshape(span, HD)
    value = tiles[buf, :, :, :, HD:].reshape(span, HD)
    query = query_ref[0]
    scores = lax.dot_general(
        query, key, (((1,), (1,)), ((), ())), preferred_element_type=jnp.float32
    ) * (HD ** -0.5)
    step = lax.rem(lax.broadcasted_iota(jnp.int32, (GH * STEPS, span), 0), STEPS)
    where = lax.broadcasted_iota(jnp.int32, (GH * STEPS, span), 1)
    scores = jnp.where(where < length + step + 1, scores, -jnp.inf)
    highest = jnp.max(scores, axis=1, keepdims=True)
    weights = jnp.exp(scores - highest)
    totals = jnp.sum(weights, axis=1, keepdims=True)
    probs = (weights / totals).astype(jnp.bfloat16)
    mixed = jnp.dot(probs, value, preferred_element_type=jnp.float32).astype(jnp.bfloat16)
    for g in range(GH):
        out_ref[0, :, g * HD:(g + 1) * HD] = mixed[g * STEPS:(g + 1) * STEPS]

    @pl.when(slot == REQ_G - 1)
    def _():
        for which in (REQ_G - 2, REQ_G - 1):
            for j in range(MAXP):
                page_copy(jnp.int32(which), j).wait()


def serve(slot_len, table, arrived, queries, new_kv):
    return pl.pallas_call(
        serve_kernel,
        grid_spec=pltpu.PrefetchScalarGridSpec(
            num_scalar_prefetch=2,
            grid=(REQ_G,),
            in_specs=[
                pl.BlockSpec((GROUPS, 1, MAXP, ROWS, HD), lambda i, *_: (0, i, 0, 0, 0)),
                pl.BlockSpec((1, GH * STEPS, HD), lambda i, *_: (i, 0, 0)),
                pl.BlockSpec((1, STEPS, 2 * HD), lambda i, *_: (i, 0, 0)),
            ],
            out_specs=[
                pl.BlockSpec(memory_space=pl.ANY),
                pl.BlockSpec((1, STEPS, GH * HD), lambda i, *_: (i, 0, 0)),
            ],
            scratch_shapes=[
                pltpu.VMEM((2, MAXP, ROW_TILES, ROWS, 2 * HD), jnp.bfloat16),
                pltpu.SemaphoreType.DMA((2, MAXP)),
            ],
        ),
        out_shape=[
            jax.ShapeDtypeStruct((ENTRIES, ROW_TILES, ROWS, 2 * HD), jnp.bfloat16),
            jax.ShapeDtypeStruct((REQ_G, STEPS, GH * HD), jnp.bfloat16),
        ],
        compiler_params=pltpu.CompilerParams(vmem_limit_bytes=40 * 1024 * 1024),
        name="serve",
    )(slot_len, table, arrived, queries, new_kv)


def table_tile(lengths, owner_table, decode_slot):
    place = (owner_table // PAGES_D) * TILES + owner_table % PAGES_D
    facts = jnp.stack(
        [lengths % PAGE, lengths // PAGE, decode_slot // REQ_G, decode_slot % REQ_G], axis=0
    )
    facts = jnp.pad(facts, ((0, ROWS - 4), (0, HD - 2 * REQ_G)))
    return jnp.concatenate([place.T, facts], axis=1).astype(jnp.bfloat16)


def shards(fresh, lengths, owner_table, decode_slot, decode_table, queries, new_kv):
    meta = table_tile(lengths, owner_table, decode_slot)
    sent = cut(fresh.reshape(PAGES_D, KVH, ROW_TILES, ROWS, 2 * HD), meta)
    got = lax.all_to_all(sent, ("group", "tp"), split_axis=0, concat_axis=0, tiled=True)
    packed, all_len = pick(got.reshape(GROUPS * TP * TILES, ROWS, HD))
    arrived = lax.all_to_all(
        packed.reshape(GROUPS, ENTRIES, ROWS, HD), "group", split_axis=0, concat_axis=0, tiled=True
    )
    slot_len = lax.dynamic_slice_in_dim(all_len, lax.axis_index("group") * REQ_G, REQ_G, 0)
    by_head = queries.reshape(REQ_G, STEPS, GH, HD).transpose(0, 2, 1, 3)
    pool, attended = serve(
        slot_len,
        decode_table.reshape(-1),
        arrived.reshape(GROUPS, REQ_G, MAXP, ROWS, HD),
        by_head.reshape(REQ_G, GH * STEPS, HD),
        new_kv,
    )
    return pool.reshape(ENTRIES, 1, PAGE, 2 * HD), attended


def solution(mesh):
    return jax.shard_map(
        shards,
        mesh=mesh,
        in_specs=(
            P(("group", "tp"), None, None, None),
            P("group"),
            P("group", None),
            P("group"),
            P("group", None),
            P("group", None, "tp"),
            P("group", None, "tp"),
        ),
        out_specs=(P("group", "tp", None, None), P("group", None, "tp")),
        check_vma=False,
    )
```

time: 249 us -> 157 us (0.63)
  waiting for transfers between devices: 157 us -> 63 us
  blocking collectives: 0 us -> 55.6 us
  local copies, waits for them, and re-layouts: 51.2 us -> 2.26 us
  Pallas kernels: 0 us -> 28.4 us
  starting transfers between devices: 19.9 us -> 4.67 us
  other arithmetic: 14.5 us -> 2.06 us
  matrix products: 4.6 us -> 0 us
    all_to_all x3 -> x1, waiting for transfers between devices: 157 us -> 63 us  [shards(): lax.all_to_all(packed.reshape(GROUPS, ENTRIES, ROWS, HD), 'group', split_...]
    all_to_all x0 -> x1, blocking collectives: none -> 55.6 us  [shards(): lax.all_to_all(sent, ('group', 'tp'), split_axis=0, concat_axis=0, tiled=...]
    pallas_call x0 -> x3, Pallas kernels: none -> 28.4 us  [the longest x1 15.2 us: serve(): pl.pallas_call(serve_kernel, grid_spec=pltpu.PrefetchScalarGridSpec(num_s...]
    scatter x2 -> x0, local copies, waits for them, and re-layouts: 27.4 us -> none  [the longest x1 19.3 us: shards(): page_pool = jnp.zeros(flat_shape, slot_tiles.dtype).at[decode_table.resha...]
    gather x3 -> x0, local copies, waits for them, and re-layouts: 15.3 us -> none  [the longest x1 8.51 us: page_tiles(): jnp.take(page_store, table_rows.reshape(-1), axis=0).reshape(shaped)]
    all_to_all x3 -> x1, starting transfers between devices: 19.9 us -> 4.67 us  [shards(): lax.all_to_all(packed.reshape(GROUPS, ENTRIES, ROWS, HD), 'group', split_...]
    select_n x8 -> x0, other arithmetic: 12.7 us -> none  [the longest x1 8.1 us: token_mask(): jnp.where(inside[:, :, None, :, None], tile_set, jnp.zeros((), tile_set.d...]
    dot_general x2 -> x0, matrix products: 4.6 us -> none  [the longest x1 3.85 us: attend(): jnp.einsum('rskgd,rjkpd->rkgsjp', shaped, key_part, preferred_element_typ...]
  transfers between devices with their start and end apart: 3 -> 1, of which waited for: 2 -> 1; matrix products, arithmetic and copies ran while one was open for 8% -> 0% of each run, Pallas kernels for 0% -> 0%
where the time goes in v1:
time: 157 us
  waiting for transfers between devices  63 us (40%)
  blocking collectives  55.6 us (35%)
  Pallas kernels  28.4 us (18%)
  starting transfers between devices  4.67 us (3%)
  local copies, waits for them, and re-layouts  2.26 us (1%)
  other arithmetic  2.06 us (1%)
    all_to_all x1, waiting for transfers between devices, shards(): lax.all_to_all(packed.reshape(GROUPS, ENTRIES, ROWS, HD), 'group', split_...  63 us
    all_to_all x1, blocking collectives, shards(): lax.all_to_all(sent, ('group', 'tp'), split_axis=0, concat_axis=0, tiled=...  55.6 us
    pallas_call x1, Pallas kernels, serve(): pl.pallas_call(serve_kernel, grid_spec=pltpu.PrefetchScalarGridSpec(num_s...  15.2 us
    pallas_call x1, Pallas kernels, pick(): pl.pallas_call(pick_kernel, in_specs=[pl.BlockSpec(memory_space=pltpu.VME...  6.79 us
    pallas_call x1, Pallas kernels, cut(): pl.pallas_call(cut_kernel, grid=(ROW_TILES,), in_specs=[pl.BlockSpec((PAG...  6.35 us
    all_to_all x1, starting transfers between devices, shards(): lax.all_to_all(packed.reshape(GROUPS, ENTRIES, ROWS, HD), 'group', split_...  4.67 us
  transfers between devices with their start and end apart: 1, of which 1 were waited for; matrix products, arithmetic and copies ran while one was open for 0% of the time, Pallas kernels for 0%

profile of v1, /device:TPU:0, one launch (start us, length us, event | category | flops | bytes accessed | tf_op | source)
XLA Modules:
  0.0 156.6 jit_solution(8028226096952946864)
XLA Ops:
  0.6 0.7 fusion.16
  1.3 0.7 fusion.18
  2.0 0.7 pad_maximum_fusion.meta_ref
  2.7 6.3 %cut.1 = bf16[128,13,8,128]{3,2,1,0:T(8,128)(2,1)} custom-call(bf16[12,8,8,8,256]{4,3,2,1,0:T(8,128)(2,1)} %bitcast.25, bf16[8,128]{1,0:T(8,128)(2,1)} %pad_maximum_fusion.meta_ref), custom_call_target="tpu_custom_call" | custom-call | tf_op jit(solution)/shard_map/cut/pallas_call | solution.py:37
  9.0 55.6 %all_to_all.10 = bf16[128,13,8,128]{3,2,1,0:T(8,128)(2,1)S(1)} all-to-all(bf16[128,13,8,128]{3,2,1,0:T(8,128)(2,1)} %cut.1), channel_id=1, replica_groups=mesh['group'=16,'tp'=8] {'group','tp'}, dimensions={0} | all-to-all | bytes 6815744 | tf_op jit(solution)/shard_map/all_to_all | solution.py:190
  64.6 6.8 %pick.1 = (bf16[2048,8,128]{2,1,0:T(8,128)(2,1)S(1)}, s32[256]{0:T(256)S(1)}) custom-call(bf16[1664,8,128]{2,1,0:T(8,128)(2,1)S(1)} %bitcast.22), custom_call_target="tpu_custom_call" | custom-call | tf_op jit(solution)/shard_map/pick/pallas_call | solution.py:72
  71.4 0.0 copy-start
  71.4 2.0 %copy-done = bf16[2048,8,128]{2,1,0:T(8,128)(2,1)} copy-done((bf16[2048,8,128]{2,1,0:T(8,128)(2,1)}, bf16[2048,8,128]{2,1,0:T(8,128)(2,1)S(1)}, u32[]{:S(2)}) %copy-start) | copy-done | bytes 4194328
  73.4 0.0 copy-start.3
  73.4 0.0 copy-start.1
  73.4 0.0 copy-start.2
  73.4 4.7 %all-to-all-start.1 = ((bf16[16,128,8,128]{3,2,1,0:T(8,128)(2,1)}), bf16[16,128,8,128]{3,2,1,0:T(8,128)(2,1)}, u32[]{:S(2)}, u32[]{:S(2)}) async-start(bf16[16,128,8,128]{3,2,1,0:T(8,128)(2,1)} %bitcast.23), calls=%async_computation.1 | async-start | bytes 8388608 | tf_op jit(solution)/shard_map/all_to_all | solution.py:192
  78.1 0.0 copy-done.3
  78.1 0.1 copy.12
  78.2 0.1 reshape.30.table_ref
  78.3 0.1 dynamic_slice.3.len_ref
  78.4 63.0 %all-to-all-done.1 = bf16[16,128,8,128]{3,2,1,0:T(8,128)(2,1)} async-done(((bf16[16,128,8,128]{3,2,1,0:T(8,128)(2,1)}), bf16[16,128,8,128]{3,2,1,0:T(8,128)(2,1)}, u32[]{:S(2)}, u32[]{:S(2)}) %all-to-all-start.1) | async-done | bytes 4194336 | tf_op jit(solution)/shard_map/all_to_all | solution.py:192
  141.4 0.0 copy-done.1
  141.4 0.0 copy-done.2
  141.4 15.2 %serve.1 = (bf16[128,8,8,256]{3,2,1,0:T(8,128)(2,1)}, bf16[16,4,1024]{2,1,0:T(4,128)(2,1)}) custom-call(s32[16]{0:T(128)S(1)} %dynamic_slice.3.len_ref, s32[128]{0:T(128)S(1)} %reshape.30.table_ref, bf16[16,16,8,8,128]{4,3,2,1,0:T(8,128)(2,1)} %bitcast.8.arrived_ref, bf16[16,32,128]{2,1,0:T(8,128)(2,1)S(1)} %bitcast.24, bf16[16,4,256]{2,1,0:T(4,128)(2,1)S(1)} %copy-done.2), custom_call_target="tpu_custom_call" | custom-call | tf_op jit(solution)/shard_map/serve/pallas_call | solution.py:150
  (1 shorter events, 0.0 us)
Async XLA Ops:
  71.4 2.0 %copy-start = (bf16[2048,8,128]{2,1,0:T(8,128)(2,1)}, bf16[2048,8,128]{2,1,0:T(8,128)(2,1)S(1)}, u32[]{:S(2)}) copy-start(bf16[2048,8,128]{2,1,0:T(8,128)(2,1)S(1)} %get-tuple-element.7) | copy-start | bytes 12582916
  73.4 4.7 %copy-start.3 = (s32[16,8]{0,1:T(8,128)S(1)}, s32[16,8]{0,1:T(8,128)}, u32[]{:S(2)}) copy-start(s32[16,8]{0,1:T(8,128)} %param.11) | copy-start | bytes 1540
  73.4 67.9 %copy-start.1 = (bf16[16,4,1024]{2,1,0:T(4,128)(2,1)S(1)}, bf16[16,4,1024]{2,1,0:T(4,128)(2,1)}, u32[]{:S(2)}) copy-start(bf16[16,4,1024]{2,1,0:T(4,128)(2,1)} %param.12) | copy-start | bytes 393220
  73.4 67.9 %copy-start.2 = (bf16[16,4,256]{2,1,0:T(4,128)(2,1)S(1)}, bf16[16,4,256]{2,1,0:T(4,128)(2,1)}, u32[]{:S(2)}) copy-start(bf16[16,4,256]{2,1,0:T(4,128)(2,1)} %new_ref.1) | copy-start | bytes 98308
  73.4 67.9 %all-to-all-start.1 = ((bf16[16,128,8,128]{3,2,1,0:T(8,128)(2,1)}), bf16[16,128,8,128]{3,2,1,0:T(8,128)(2,1)}, u32[]{:S(2)}, u32[]{:S(2)}) async-start(bf16[16,128,8,128]{3,2,1,0:T(8,128)(2,1)} %bitcast.23), calls=%async_computation.1 | async-start | bytes 8388608 | tf_op jit(solution)/shard_map/all_to_all | solution.py:192

commit v2 on v1

v2 whole, which is shorter than its diff:
```python
import jax
import jax.numpy as jnp
from jax import lax
from jax.experimental import pallas as pl
from jax.experimental.pallas import tpu as pltpu
from jax.sharding import PartitionSpec as P

HEADS = 64
KVH = 8
HD = 128
PAGE = 64
STEPS = 4
MAXP = 8
REQ_G = 16
GROUPS = 16
TP = 8
PAGES_D = 12
ROWS = 8
ROW_TILES = PAGE // ROWS
TILES = PAGES_D + 1
ENTRIES = REQ_G * MAXP
GH = HEADS // KVH
SPAN = MAXP * PAGE
UNROLL = 8

VMEM = pl.BlockSpec(memory_space=pltpu.VMEM)
SMEM = pl.BlockSpec(memory_space=pltpu.SMEM)
HBM = pl.BlockSpec(memory_space=pltpu.HBM)
ANY = pl.BlockSpec(memory_space=pl.ANY)
LIMIT = 40 * 1024 * 1024


def cut_kernel(fresh_ref, owner_ref, length_ref, slot_ref, out_ref, pages, owners, facts, ints, sems, table_sem):
    copies = []
    for page in range(PAGES_D):
        copy = pltpu.make_async_copy(fresh_ref.at[page], pages.at[page], sems.at[page])
        copy.start()
        copies.append(copy)
    tables = [
        pltpu.make_async_copy(owner_ref, owners, table_sem.at[0]),
        pltpu.make_async_copy(length_ref, facts.at[0], table_sem.at[1]),
        pltpu.make_async_copy(slot_ref, facts.at[1], table_sem.at[2]),
    ]
    for copy in tables:
        copy.start()

    for page in range(PAGES_D):
        copies[page].wait()
        for rt in range(ROW_TILES):
            for half in range(2):
                for head in range(KVH):
                    row = (rt * 2 + half) * KVH + head
                    out_ref[row, page] = pages[page, head, rt, :, half * HD:(half + 1) * HD]

    for copy in tables:
        copy.wait()
    owner = owners[...]
    device = (owner * 43) >> 9
    place = device * TILES + (owner - device * PAGES_D)
    length = facts[0]
    ints[...] = jnp.zeros_like(ints)
    for j in range(MAXP):
        ints[0:1, j * REQ_G:(j + 1) * REQ_G] = place[j:j + 1, :]
    ints[1:2, :REQ_G] = length & (PAGE - 1)
    ints[2:3, :REQ_G] = length >> 6
    ints[3:4, :REQ_G] = facts[1]
    tile = ints[...].astype(jnp.float32).astype(jnp.bfloat16)
    for row in range(GROUPS * TP):
        out_ref[row, PAGES_D] = tile


def cut(fresh, owner_table, lengths, decode_slot):
    return pl.pallas_call(
        cut_kernel,
        in_specs=[HBM, HBM, HBM, HBM],
        out_specs=VMEM,
        out_shape=jax.ShapeDtypeStruct((GROUPS * TP, TILES, ROWS, HD), jnp.bfloat16),
        scratch_shapes=[
            pltpu.VMEM((PAGES_D, KVH, ROW_TILES, ROWS, 2 * HD), jnp.bfloat16),
            pltpu.VMEM((MAXP, REQ_G), jnp.int32),
            pltpu.VMEM((2, 1, REQ_G), jnp.int32),
            pltpu.VMEM((ROWS, HD), jnp.int32),
            pltpu.SemaphoreType.DMA((PAGES_D,)),
            pltpu.SemaphoreType.DMA((3,)),
        ],
        compiler_params=pltpu.CompilerParams(vmem_limit_bytes=LIMIT),
        name="cut",
    )(
        fresh.reshape(PAGES_D, KVH, ROW_TILES, ROWS, 2 * HD),
        owner_table.T,
        lengths.reshape(1, REQ_G),
        decode_slot.reshape(1, REQ_G),
    )


def pick_kernel(got_ref, out_ref, len_ref, ints, table, sem):
    for home in range(GROUPS):
        tile = got_ref[home * TP * TILES + PAGES_D].astype(jnp.float32).astype(jnp.int32)
        ints[home:home + 1, :] = tile[0:1] + home * TP * TILES
        ints[GROUPS + home:GROUPS + home + 1, :] = tile[1:2] + tile[2:3] * PAGE
        ints[2 * GROUPS + home:2 * GROUPS + home + 1, :] = tile[3:4]
    copy = pltpu.make_async_copy(ints, table, sem)
    copy.start()
    copy.wait()

    def one_home(home, carry):
        for item in range(REQ_G):
            slot = table[home + 2 * GROUPS, item]
            len_ref[slot] = table[home + GROUPS, item]
            for j in range(MAXP):
                out_ref[slot * MAXP + j] = got_ref[table[home, j * REQ_G + item]]
        return carry

    lax.fori_loop(0, GROUPS, one_home, 0)


def pick(got):
    return pl.pallas_call(
        pick_kernel,
        in_specs=[VMEM],
        out_specs=[VMEM, SMEM],
        out_shape=[
            jax.ShapeDtypeStruct((GROUPS * ENTRIES, ROWS, HD), jnp.bfloat16),
            jax.ShapeDtypeStruct((GROUPS * REQ_G,), jnp.int32),
        ],
        scratch_shapes=[
            pltpu.VMEM((3 * GROUPS, HD), jnp.int32),
            pltpu.SMEM((3 * GROUPS, HD), jnp.int32),
            pltpu.SemaphoreType.DMA,
        ],
        compiler_params=pltpu.CompilerParams(vmem_limit_bytes=LIMIT),
        name="pick",
    )(got)


def serve_kernel(len_ref, table_ref, arrived_ref, query_ref, new_ref, pool_ref, out_ref, tiles, sems):
    mine = lax.axis_index("group") * REQ_G

    def page_copy(slot, j):
        return pltpu.make_async_copy(
            tiles.at[slot, j], pool_ref.at[table_ref[j, slot]], sems.at[slot, j]
        )

    row = lax.broadcasted_iota(jnp.int32, (ROWS, HD), 0)
    wide = lax.broadcasted_iota(jnp.int32, (ROWS, 2 * HD), 0)

    def fill(slot, carry):
        length = len_ref[mine + slot]
        for j in range(MAXP):
            for rt in range(ROW_TILES):
                old = row < length - (j * PAGE + rt * ROWS)
                for half in range(2):
                    x = arrived_ref[2 * rt + half, slot, j].astype(jnp.float32)
                    x = jnp.where(old, x, 0.0).astype(jnp.bfloat16)
                    tiles[slot, j, rt, :, half * HD:(half + 1) * HD] = x
        late = new_ref[slot].astype(jnp.float32)
        for position in (length, length + STEPS - 1):
            j, rt = position // PAGE, position % PAGE // ROWS
            at = wide + (position // ROWS * ROWS - length)
            x = tiles[slot, j, rt].astype(jnp.float32)
            for u in range(STEPS):
                x = jnp.where(at == u, late[u:u + 1], x)
            tiles[slot, j, rt] = x.astype(jnp.bfloat16)
        for j in range(MAXP):
            page_copy(slot, j).start()
        return carry

    lax.fori_loop(0, REQ_G, fill, 0)

    shape = (GH * STEPS, SPAN)
    step = lax.rem(lax.broadcasted_iota(jnp.int32, shape, 0), STEPS)
    ahead = lax.broadcasted_iota(jnp.int32, shape, 1) - step - 1

    def attend(first, carry):
        slots = [first * UNROLL + k for k in range(UNROLL)]
        scores = []
        for slot in slots:
            key = tiles[slot, :, :, :, :HD].reshape(SPAN, HD)
            products = lax.dot_general(
                query_ref[slot], key, (((1,), (1,)), ((), ())), preferred_element_type=jnp.float32
            )
            scores.append(jnp.where(ahead < len_ref[mine + slot], products * (HD ** -0.5), -jnp.inf))
        highest = [jnp.max(x, axis=1, keepdims=True) for x in scores]
        weights = [jnp.exp(x - y) for x, y in zip(scores, highest)]
        totals = [jnp.sum(x, axis=1, keepdims=True) for x in weights]
        probs = [(x / y).astype(jnp.bfloat16) for x, y in zip(weights, totals)]
        for slot, prob in zip(slots, probs):
            value = tiles[slot, :, :, :, HD:].reshape(SPAN, HD)
            mixed = jnp.dot(prob, value, preferred_element_type=jnp.float32).astype(jnp.bfloat16)
            for g in range(GH):
                out_ref[slot, :, g * HD:(g + 1) * HD] = mixed[g * STEPS:(g + 1) * STEPS]
        return carry

    lax.fori_loop(0, REQ_G // UNROLL, attend, 0)

    def finish(slot, carry):
        for j in range(MAXP):
            page_copy(slot, j).wait()
        return carry

    lax.fori_loop(0, REQ_G, finish, 0)


def serve(lengths, table, arrived, queries, new_kv):
    return pl.pallas_call(
        serve_kernel,
        in_specs=[SMEM, SMEM, VMEM, VMEM, VMEM],
        out_specs=[ANY, VMEM],
        out_shape=[
            jax.ShapeDtypeStruct((ENTRIES, ROW_TILES, ROWS, 2 * HD), jnp.bfloat16),
            jax.ShapeDtypeStruct((REQ_G, STEPS, GH * HD), jnp.bfloat16),
        ],
        scratch_shapes=[
            pltpu.VMEM((REQ_G, MAXP, ROW_TILES, ROWS, 2 * HD), jnp.bfloat16),
            pltpu.SemaphoreType.DMA((REQ_G, MAXP)),
        ],
        compiler_params=pltpu.CompilerParams(vmem_limit_bytes=LIMIT),
        name="serve",
    )(lengths, table, arrived, queries, new_kv)


def shards(fresh, lengths, owner_table, decode_slot, decode_table, queries, new_kv):
    sent = cut(fresh, owner_table, lengths, decode_slot)
    got = lax.all_to_all(sent, ("group", "tp"), split_axis=0, concat_axis=0, tiled=True)
    packed, all_len = pick(got.reshape(GROUPS * TP * TILES, ROWS, HD))
    by_head = queries.reshape(REQ_G, STEPS, GH, HD).transpose(0, 2, 1, 3)
    arrived = lax.all_to_all(
        packed.reshape(GROUPS, ENTRIES, ROWS, HD), "group", split_axis=0, concat_axis=0, tiled=True
    )
    pool, attended = serve(
        all_len,
        decode_table.T,
        arrived.reshape(GROUPS, REQ_G, MAXP, ROWS, HD),
        by_head.reshape(REQ_G, GH * STEPS, HD),
        new_kv,
    )
    return pool.reshape(ENTRIES, 1, PAGE, 2 * HD), attended


def solution(mesh):
    return jax.shard_map(
        shards,
        mesh=mesh,
        in_specs=(
            P(("group", "tp"), None, None, None),
            P("group"),
            P("group", None),
            P("group"),
            P("group", None),
            P("group", None, "tp"),
            P("group", None, "tp"),
        ),
        out_specs=(P("group", "tp", None, None), P("group", None, "tp")),
        check_vma=False,
    )
```

time: 157 us -> 125 us (0.80)
  waiting for transfers between devices: 63 us -> 0 us
  blocking collectives: 55.6 us -> 109 us
  Pallas kernels: 28.4 us -> 11.4 us
  starting transfers between devices: 4.67 us -> 0 us
  other arithmetic: 2.06 us -> 0 us
  local copies, waits for them, and re-layouts: 2.26 us -> 3.9 us
    all_to_all x1 -> x0, waiting for transfers between devices: 63 us -> none  [shards(): lax.all_to_all(packed.reshape(GROUPS, ENTRIES, ROWS, HD), 'group', split_...]
    all_to_all x0 -> x1, blocking collectives: none -> 53.7 us  [shards(): lax.all_to_all(packed.reshape(GROUPS, ENTRIES, ROWS, HD), 'group', split_...]
    pallas_call x3, Pallas kernels: 28.4 us -> 11.4 us  [the longest x1 5.9 us: serve(): pl.pallas_call(serve_kernel, in_specs=[SMEM, SMEM, VMEM, VMEM, VMEM], out...]
    all_to_all x1 -> x0, starting transfers between devices: 4.67 us -> none  [shards(): lax.all_to_all(packed.reshape(GROUPS, ENTRIES, ROWS, HD), 'group', split_...]
    unnamed x9 -> x14, local copies, waits for them, and re-layouts: 2.09 us -> 3.9 us
  transfers between devices with their start and end apart: 1 -> 0, of which waited for: 1 -> 0; matrix products, arithmetic and copies ran while one was open for 0% -> 0% of each run, Pallas kernels for 0% -> 0%
where the time goes in v2:
time: 125 us
  blocking collectives  109 us (87%)
  Pallas kernels  11.4 us (9%)
  local copies, waits for them, and re-layouts  3.9 us (3%)
    all_to_all x1, blocking collectives, shards(): lax.all_to_all(sent, ('group', 'tp'), split_axis=0, concat_axis=0, tiled=...  55.4 us
    all_to_all x1, blocking collectives, shards(): lax.all_to_all(packed.reshape(GROUPS, ENTRIES, ROWS, HD), 'group', split_...  53.7 us
    pallas_call x1, Pallas kernels, serve(): pl.pallas_call(serve_kernel, in_specs=[SMEM, SMEM, VMEM, VMEM, VMEM], out...  5.9 us
    pallas_call x1, Pallas kernels, pick(): pl.pallas_call(pick_kernel, in_specs=[VMEM], out_specs=[VMEM, SMEM], out_...  4.44 us
    unnamed x14, local copies, waits for them, and re-layouts  3.9 us

profile of v2, /device:TPU:0, one launch (start us, length us, event | category | flops | bytes accessed | tf_op | source)
XLA Modules:
  0.0 125.1 jit_solution(6450759132698396765)
XLA Ops:
  0.6 0.0 copy-start
  0.6 1.9 %copy-done = bf16[12,8,64,256]{3,2,1,0:T(8,128)(2,1)S(1)} copy-done((bf16[12,8,64,256]{3,2,1,0:T(8,128)(2,1)S(1)}, bf16[12,8,64,256]{3,2,1,0:T(8,128)(2,1)}, u32[]{:S(2)}) %copy-start) | copy-done | bytes 3145752
  2.5 0.0 copy-start.3
  2.5 0.7 copy-done.3
  3.2 0.0 copy-start.5
  3.2 0.7 copy-done.5
  3.9 0.0 copy-start.6
  3.9 0.7 copy-done.6
  4.5 1.1 cut.1
  5.6 55.4 %all_to_all.10 = bf16[128,13,8,128]{3,2,1,0:T(8,128)(2,1)S(1)} all-to-all(bf16[128,13,8,128]{3,2,1,0:T(8,128)(2,1)S(1)} %cut.1), channel_id=1, replica_groups=mesh['group'=16,'tp'=8] {'group','tp'}, dimensions={0} | all-to-all | bytes 6815744 | tf_op jit(solution)/shard_map/all_to_all | solution.py:224
  61.0 4.4 %pick.1 = (bf16[2048,8,128]{2,1,0:T(8,128)(2,1)S(1)}, s32[256]{0:T(256)S(1)}) custom-call(bf16[1664,8,128]{2,1,0:T(8,128)(2,1)S(1)} %bitcast.17), custom_call_target="tpu_custom_call" | custom-call | tf_op jit(solution)/shard_map/pick/pallas_call | solution.py:118
  65.4 0.0 copy-start.1
  65.4 0.0 copy-start.2
  65.4 0.0 copy-start.4
  65.4 53.7 %all_to_all.11 = bf16[16,128,8,128]{3,2,1,0:T(8,128)(2,1)S(1)} all-to-all(bf16[16,128,8,128]{3,2,1,0:T(8,128)(2,1)S(1)} %bitcast.18), channel_id=1, replica_groups=mesh['group'=16,'tp'=8] {'group'}, dimensions={0} | all-to-all | bytes 8388608 | tf_op jit(solution)/shard_map/all_to_all | solution.py:227
  119.2 0.0 copy-done.1
  119.2 0.0 copy-done.2
  119.2 0.0 copy-done.4
  119.2 5.9 %serve.1 = (bf16[128,8,8,256]{3,2,1,0:T(8,128)(2,1)}, bf16[16,4,1024]{2,1,0:T(4,128)(2,1)}) custom-call(s32[256]{0:T(256)S(1)} %get-tuple-element.6.len_ref, s32[8,16]{1,0:T(8,128)S(1)} %bitcast.22, bf16[16,16,8,8,128]{4,3,2,1,0:T(8,128)(2,1)S(1)} %bitcast.16, bf16[16,32,128]{2,1,0:T(8,128)(2,1)S(1)} %bitcast.20, bf16[16,4,256]{2,1,0:T(4,128)(2,1)S(1)} %copy-done.2), custom_call_target="tpu_custom_call" | custom-call | tf_op jit(solution)/shard_map/serve/pallas_call | solution.py:205
Async XLA Ops:
  0.6 1.9 %copy-start = (bf16[12,8,64,256]{3,2,1,0:T(8,128)(2,1)S(1)}, bf16[12,8,64,256]{3,2,1,0:T(8,128)(2,1)}, u32[]{:S(2)}) copy-start(bf16[12,8,64,256]{3,2,1,0:T(8,128)(2,1)} %param.7) | copy-start | bytes 9437188
  2.5 0.7 copy-start.3
  3.2 0.7 copy-start.5
  3.9 0.7 copy-start.6
  65.4 53.8 %copy-start.1 = (bf16[16,4,1024]{2,1,0:T(4,128)(2,1)S(1)}, bf16[16,4,1024]{2,1,0:T(4,128)(2,1)}, u32[]{:S(2)}) copy-start(bf16[16,4,1024]{2,1,0:T(4,128)(2,1)} %param.12) | copy-start | bytes 393220
  65.4 53.8 %copy-start.2 = (bf16[16,4,256]{2,1,0:T(4,128)(2,1)S(1)}, bf16[16,4,256]{2,1,0:T(4,128)(2,1)}, u32[]{:S(2)}) copy-start(bf16[16,4,256]{2,1,0:T(4,128)(2,1)} %new_ref.1) | copy-start | bytes 98308
  65.4 53.7 %copy-start.4 = (s32[16,8]{0,1:T(8,128)S(1)}, s32[16,8]{0,1:T(8,128)}, u32[]{:S(2)}) copy-start(s32[16,8]{0,1:T(8,128)} %param.11) | copy-start | bytes 1540

commit v3 on v2

v3 whole, which is shorter than its diff:
```python
import functools

import jax
import jax.numpy as jnp
from jax import lax
from jax.experimental import pallas as pl
from jax.experimental.pallas import tpu as pltpu
from jax.sharding import PartitionSpec as P

HEADS = 64
KVH = 8
HD = 128
PAGE = 64
STEPS = 4
MAXP = 8
REQ_G = 16
GROUPS = 16
TP = 8
PAGES_D = 12
ROWS = 8
ROW_TILES = PAGE // ROWS
TILES = PAGES_D + 1
ENTRIES = REQ_G * MAXP
GH = HEADS // KVH
BLOCKS = HD // REQ_G
SLOTS = GROUPS * REQ_G
SPAN = MAXP * PAGE
USUAL = 108
UNROLL = 8

VMEM = pl.BlockSpec(memory_space=pltpu.VMEM)
SMEM = pl.BlockSpec(memory_space=pltpu.SMEM)
HBM = pl.BlockSpec(memory_space=pltpu.HBM)
ANY = pl.BlockSpec(memory_space=pl.ANY)
LIMIT = 40 * 1024 * 1024


def cut_kernel(fresh_ref, owner_ref, length_ref, slot_ref, out_ref, pages, owners, facts, ints, sems, table_sem):
    copies = []
    for page in range(PAGES_D):
        copy = pltpu.make_async_copy(fresh_ref.at[page], pages.at[page], sems.at[page])
        copy.start()
        copies.append(copy)
    tables = [
        pltpu.make_async_copy(owner_ref, owners, table_sem.at[0]),
        pltpu.make_async_copy(length_ref, facts.at[0], table_sem.at[1]),
        pltpu.make_async_copy(slot_ref, facts.at[1], table_sem.at[2]),
    ]
    for copy in tables:
        copy.start()

    for page in range(PAGES_D):
        copies[page].wait()
        for rt in range(ROW_TILES):
            for half in range(2):
                for head in range(KVH):
                    row = (rt * 2 + half) * KVH + head
                    out_ref[row, page] = pages[page, head, rt, :, half * HD:(half + 1) * HD]

    for copy in tables:
        copy.wait()
    owner = owners[...]
    device = (owner * 43) >> 9
    place = device * TILES + (owner - device * PAGES_D)
    length = facts[0]
    ints[...] = jnp.zeros_like(ints)
    for block in range(BLOCKS):
        lanes = slice(block * REQ_G, (block + 1) * REQ_G)
        ints[:ROWS, lanes] = place
        ints[ROWS:ROWS + 1, lanes] = length & (PAGE - 1)
        ints[ROWS + 1:ROWS + 2, lanes] = length >> 6
        ints[ROWS + 2:ROWS + 3, lanes] = facts[1]
    block = lax.broadcasted_iota(jnp.int32, (ROWS, HD), 1) // REQ_G
    mine = lax.rem(lax.axis_index("group"), BLOCKS)
    tile = jnp.where(block == mine, ints[:ROWS], 0)
    tile = jnp.where(block == lax.rem(mine + 1, BLOCKS), ints[ROWS:], tile)
    tile = tile.astype(jnp.float32).astype(jnp.bfloat16)
    for row in range(GROUPS * TP):
        out_ref[row, PAGES_D] = tile


def cut(fresh, owner_table, lengths, decode_slot):
    return pl.pallas_call(
        cut_kernel,
        in_specs=[HBM, HBM, HBM, HBM],
        out_specs=VMEM,
        out_shape=jax.ShapeDtypeStruct((GROUPS * TP, TILES, ROWS, HD), jnp.bfloat16),
        scratch_shapes=[
            pltpu.VMEM((PAGES_D, KVH, ROW_TILES, ROWS, 2 * HD), jnp.bfloat16),
            pltpu.VMEM((MAXP, REQ_G), jnp.int32),
            pltpu.VMEM((2, 1, REQ_G), jnp.int32),
            pltpu.VMEM((2 * ROWS, HD), jnp.int32),
            pltpu.SemaphoreType.DMA((PAGES_D,)),
            pltpu.SemaphoreType.DMA((3,)),
        ],
        compiler_params=pltpu.CompilerParams(vmem_limit_bytes=60078000),
        name="cut",
    )(
        fresh.reshape(PAGES_D, KVH, ROW_TILES, ROWS, 2 * HD),
        owner_table.T,
        lengths.reshape(1, REQ_G),
        decode_slot.reshape(1, REQ_G),
    )


def pick_kernel(cap, got_ref, out_ref, len_ref, over_ref, ints, table, sem):
    block = lax.broadcasted_iota(jnp.int32, (ROWS, HD), 1) // REQ_G
    which = lax.broadcasted_iota(jnp.int32, (SLOTS, HD), 0).astype(jnp.float32)
    sorted_rows = jnp.zeros((2 * ROWS, SLOTS), jnp.float32)
    for half in range(GROUPS // BLOCKS):
        place = jnp.zeros((ROWS, HD), jnp.float32)
        facts = jnp.zeros((ROWS, HD), jnp.float32)
        for k in range(BLOCKS):
            tile = got_ref[(half * BLOCKS + k) * TP * TILES + PAGES_D].astype(jnp.float32)
            place = jnp.where(block == k, tile, place)
            facts = jnp.where(block == (k + 1) % BLOCKS, tile, facts)
        facts = pltpu.roll(facts, HD - REQ_G, 1)
        home = (block + half * BLOCKS).astype(jnp.float32)
        rows = jnp.concatenate([place, facts[0:2], home[0:6]], axis=0).astype(jnp.bfloat16)
        here = jnp.where(facts[2:3] == which, 1.0, 0.0).astype(jnp.bfloat16)
        sorted_rows += lax.dot_general(
            rows, here, (((1,), (1,)), ((), ())), preferred_element_type=jnp.float32
        )
    sorted_rows = sorted_rows.astype(jnp.int32)
    length = sorted_rows[8:9] + sorted_rows[9:10] * PAGE
    count = (length + PAGE - 1) >> 6
    slot = lax.broadcasted_iota(jnp.int32, (ROWS, SLOTS), 1)
    first = jnp.broadcast_to(count, (ROWS, SLOTS))
    for step in (1, 2, 4, 8):
        first += jnp.where(slot % REQ_G >= step, pltpu.roll(first, step, 1), 0)
    over = jnp.where(first > cap, 1.0, 0.0)
    ints[:ROWS] = sorted_rows[:ROWS] + sorted_rows[10:11] * (TP * TILES)
    ints[ROWS:] = first - count + slot // REQ_G * cap
    copy = pltpu.make_async_copy(ints, table, sem)
    copy.start()
    len_ref[...] = length
    over_ref[0] = jnp.max(over).astype(jnp.int32)
    copy.wait()

    def fill(group, clamp):
        for item in range(REQ_G):
            at = table[ROWS, group * REQ_G + item]
            for j in reversed(range(MAXP)):
                place = at + j
                if clamp:
                    place = jnp.minimum(place, GROUPS * cap - 1)
                out_ref[place] = got_ref[table[j, group * REQ_G + item]]

    def one_group(group, carry):
        fill(group, False)
        return carry

    lax.fori_loop(0, GROUPS - 1, one_group, 0)
    fill(GROUPS - 1, True)


def pick(got, cap):
    return pl.pallas_call(
        functools.partial(pick_kernel, cap),
        in_specs=[VMEM],
        out_specs=[VMEM, VMEM, SMEM],
        out_shape=[
            jax.ShapeDtypeStruct((GROUPS * cap, ROWS, HD), jnp.bfloat16),
            jax.ShapeDtypeStruct((1, SLOTS), jnp.int32),
            jax.ShapeDtypeStruct((1,), jnp.int32),
        ],
        scratch_shapes=[
            pltpu.VMEM((2 * ROWS, SLOTS), jnp.int32),
            pltpu.SMEM((2 * ROWS, SLOTS), jnp.int32),
            pltpu.SemaphoreType.DMA,
        ],
        compiler_params=pltpu.CompilerParams(vmem_limit_bytes=LIMIT),
        name="pick",
    )(got)


def serve_kernel(cap, len_ref, table_ref, arrived_ref, query_ref, new_ref, pool_ref, out_ref, tiles, sem):
    mine = lax.axis_index("group") * REQ_G

    def page_copy(slot, j):
        return pltpu.make_async_copy(
            tiles.at[slot * MAXP + j], pool_ref.at[table_ref[j, slot]], sem
        )

    row = lax.broadcasted_iota(jnp.int32, (ROWS, HD), 0)
    wide = lax.broadcasted_iota(jnp.int32, (ROWS, 2 * HD), 0)

    def fill(slot, first):
        length = len_ref[0, mine + slot]
        for j in range(MAXP):
            entry = jnp.minimum(first + j, cap - 1)
            for rt in range(ROW_TILES):
                old = row < length - (j * PAGE + rt * ROWS)
                for half in range(2):
                    x = arrived_ref[2 * rt + half, entry].astype(jnp.float32)
                    x = jnp.where(old, x, 0.0).astype(jnp.bfloat16)
                    tiles[slot * MAXP + j, rt, :, half * HD:(half + 1) * HD] = x
        late = new_ref[slot].astype(jnp.float32)
        for position in (length, length + STEPS - 1):
            j, rt = position // PAGE, position % PAGE // ROWS
            at = wide + (position // ROWS * ROWS - length)
            x = tiles[slot * MAXP + j, rt].astype(jnp.float32)
            for u in range(STEPS):
                x = jnp.where(at == u, late[u:u + 1], x)
            tiles[slot * MAXP + j, rt] = x.astype(jnp.bfloat16)
        for j in range(MAXP):
            page_copy(slot, j).start()
        return first + ((length + PAGE - 1) >> 6)

    lax.fori_loop(0, REQ_G, fill, jnp.int32(0))

    shape = (GH * STEPS, SPAN)
    step = lax.rem(lax.broadcasted_iota(jnp.int32, shape, 0), STEPS)
    ahead = lax.broadcasted_iota(jnp.int32, shape, 1) - step - 1

    def attend(first, carry):
        slots = [first * UNROLL + k for k in range(UNROLL)]
        scores = []
        for slot in slots:
            key = tiles[pl.ds(slot * MAXP, MAXP), :, :, :HD].reshape(SPAN, HD)
            products = lax.dot_general(
                query_ref[slot], key, (((1,), (1,)), ((), ())), preferred_element_type=jnp.float32
            )
            scores.append(jnp.where(ahead < len_ref[0, mine + slot], products * (HD ** -0.5), -jnp.inf))
        highest = [jnp.max(x, axis=1, keepdims=True) for x in scores]
        weights = [jnp.exp(x - y) for x, y in zip(scores, highest)]
        totals = [jnp.sum(x, axis=1, keepdims=True) for x in weights]
        probs = [(x / y).astype(jnp.bfloat16) for x, y in zip(weights, totals)]
        for slot, prob in zip(slots, probs):
            value = tiles[pl.ds(slot * MAXP, MAXP), :, :, HD:].reshape(SPAN, HD)
            mixed = jnp.dot(prob, value, preferred_element_type=jnp.float32).astype(jnp.bfloat16)
            for g in range(GH):
                out_ref[slot, :, g * HD:(g + 1) * HD] = mixed[g * STEPS:(g + 1) * STEPS]
        return carry

    lax.fori_loop(0, REQ_G // UNROLL, attend, 0)

    pltpu.make_async_copy(tiles, pool_ref, sem).wait()


def serve(lengths, table, arrived, queries, new_kv):
    return pl.pallas_call(
        functools.partial(serve_kernel, arrived.shape[1]),
        in_specs=[SMEM, SMEM, VMEM, VMEM, VMEM],
        out_specs=[ANY, VMEM],
        out_shape=[
            jax.ShapeDtypeStruct((ENTRIES, ROW_TILES, ROWS, 2 * HD), jnp.bfloat16),
            jax.ShapeDtypeStruct((REQ_G, STEPS, GH * HD), jnp.bfloat16),
        ],
        scratch_shapes=[
            pltpu.VMEM((ENTRIES, ROW_TILES, ROWS, 2 * HD), jnp.bfloat16),
            pltpu.SemaphoreType.DMA,
        ],
        compiler_params=pltpu.CompilerParams(vmem_limit_bytes=LIMIT),
        name="serve",
    )(lengths, table, arrived, queries, new_kv)


def shards(fresh, lengths, owner_table, decode_slot, decode_table, queries, new_kv):
    sent = cut(fresh, owner_table, lengths, decode_slot)
    got = lax.all_to_all(sent, ("group", "tp"), split_axis=0, concat_axis=0, tiled=True)
    got = got.reshape(GROUPS * TP * TILES, ROWS, HD)
    table = decode_table.T
    by_head = queries.reshape(REQ_G, STEPS, GH, HD).transpose(0, 2, 1, 3)
    by_head = by_head.reshape(REQ_G, GH * STEPS, HD)

    def deliver(packed, all_len, cap):
        arrived = lax.all_to_all(
            packed.reshape(GROUPS, cap, ROWS, HD), "group", split_axis=0, concat_axis=0, tiled=True
        )
        return serve(all_len, table, arrived, by_head, new_kv)

    def whole(packed, all_len):
        packed, all_len, _ = pick(got, ENTRIES)
        return deliver(packed, all_len, ENTRIES)

    packed, all_len, over = pick(got, USUAL)
    pool, attended = lax.cond(
        over[0] > 0, whole, lambda packed, all_len: deliver(packed, all_len, USUAL), packed, all_len
    )
    return pool.reshape(ENTRIES, 1, PAGE, 2 * HD), attended


def solution(mesh):
    return jax.shard_map(
        shards,
        mesh=mesh,
        in_specs=(
            P(("group", "tp"), None, None, None),
            P("group"),
            P("group", None),
            P("group"),
            P("group", None),
            P("group", None, "tp"),
            P("group", None, "tp"),
        ),
        out_specs=(P("group", "tp", None, None), P("group", None, "tp")),
        check_vma=False,
    )
```

time: 125 us -> 119 us (0.952)
  blocking collectives: 109 us -> 102 us
  local copies, waits for them, and re-layouts: 3.9 us -> 0.02 us
  Pallas kernels: 11.4 us -> 14.8 us
    all_to_all x1, blocking collectives: 53.7 us -> 46.6 us  [deliver(): lax.all_to_all(packed.reshape(GROUPS, cap, ROWS, HD), 'group', split_axis...]
    unnamed x14 -> x6, local copies, waits for them, and re-layouts: 3.9 us -> 0.02 us
    pallas_call x1, Pallas kernels: 1.05 us -> 3.9 us  [cut(): pl.pallas_call(cut_kernel, in_specs=[HBM, HBM, HBM, HBM], out_specs=VMEM,...]
where the time goes in v3:
time: 119 us; the launch traced here: 118 us
  blocking collectives  102 us (86%)
  Pallas kernels  14.8 us (12%)
  between operations  1.34 us (1%)
    all_to_all x1, blocking collectives, shards(): lax.all_to_all(sent, ('group', 'tp'), split_axis=0, concat_axis=0, tiled=...  55.6 us
    all_to_all x1, blocking collectives, deliver(): lax.all_to_all(packed.reshape(GROUPS, cap, ROWS, HD), 'group', split_axis...  46.6 us
    pallas_call x1, Pallas kernels, pick(): pl.pallas_call(functools.partial(pick_kernel, cap), in_specs=[VMEM], out_...  6.29 us
    pallas_call x1, Pallas kernels, serve(): pl.pallas_call(functools.partial(serve_kernel, arrived.shape[1]), in_spec...  4.6 us
    pallas_call x1, Pallas kernels, cut(): pl.pallas_call(cut_kernel, in_specs=[HBM, HBM, HBM, HBM], out_specs=VMEM,...  3.9 us

profile of v3, /device:TPU:0, one launch (start us, length us, event | category | flops | bytes accessed | tf_op | source)
XLA Modules:
  0.0 118.3 jit_solution(3731250854722929845)
XLA Ops:
  0.6 3.9 %cut.1 = bf16[128,13,8,128]{3,2,1,0:T(8,128)(2,1)} custom-call(bf16[12,8,8,8,256]{4,3,2,1,0:T(8,128)(2,1)} %bitcast.24, s32[8,16]{1,0:T(8,128)} %bitcast.29, s32[1,16]{1,0:T(1,128)} %bitcast.30, s32[1,16]{1,0:T(1,128)} %bitcast.31), custom_call_target="tpu_custom_call" | custom-call | tf_op jit(solution)/shard_map/cut/pallas_call | solution.py:83
  4.5 0.0 copy-start
  4.5 0.0 copy-start.1
  4.6 0.0 copy-start.2
  4.6 55.6 %all_to_all.15 = bf16[128,13,8,128]{3,2,1,0:T(8,128)(2,1)S(1)} all-to-all(bf16[128,13,8,128]{3,2,1,0:T(8,128)(2,1)} %cut.1), channel_id=1, replica_groups=mesh['group'=16,'tp'=8] {'group','tp'}, dimensions={0} | all-to-all | bytes 6815744 | tf_op jit(solution)/shard_map/all_to_all | solution.py:261
  60.2 6.3 %pick.3 = (bf16[1728,8,128]{2,1,0:T(8,128)(2,1)S(1)}, s32[1,256]{1,0:T(1,128)S(1)}, s32[1]{0:T(128)}) custom-call(bf16[1664,8,128]{2,1,0:T(8,128)(2,1)S(1)} %bitcast.21), custom_call_target="tpu_custom_call" | custom-call | tf_op jit(solution)/shard_map/pick/pallas_call | solution.py:158
  67.1 0.0 copy-done
  67.1 0.0 copy-done.1
  67.1 0.0 copy-done.2
  67.1 51.2 %conditional.1 = (bf16[16,4,1024]{2,1,0:T(4,128)(2,1)}, bf16[128,1,64,256]{3,2,1,0:T(8,128)(2,1)}) conditional(s32[]{:T(128)} %bitcast.13, (bf16[1728,8,128]{2,1,0:T(8,128)(2,1)S(1)}, s32[1,256]{1,0:T(1,128)S(1)}, s32[8,16]{1,0:T(8,128)S(1)}, bf16[16,32,128]{2,1,0:T(8,128)(2,1)S(1)}, bf16[16,4,256]{2,1,0:T(4,128)(2,1)S(1)}) %tuple.31, ...), branch_computations={%region_0.0_spmd, %region_1.0_spmd} | conditional | bytes 8388624 | solution.py:278
  67.1 46.6 %all_to_all.13.arrived_ref = bf16[16,108,8,128]{3,2,1,0:T(8,128)(2,1)S(1)} all-to-all(bf16[16,108,8,128]{3,2,1,0:T(8,128)(2,1)S(1)} %bitcast.23), channel_id=1, replica_groups=mesh['group'=16,'tp'=8] {'group'}, dimensions={0} | all-to-all | bytes 7077888 | tf_op jit(solution)/shard_map/cond/branch_0_fun/all_to_all | solution.py:268
  113.7 4.6 %serve.2 = (bf16[128,8,8,256]{3,2,1,0:T(8,128)(2,1)}, bf16[16,4,1024]{2,1,0:T(4,128)(2,1)}) custom-call(s32[1,256]{1,0:T(1,128)S(1)} %get-tuple-element.23.len_ref, s32[8,16]{1,0:T(8,128)S(1)} %get-tuple-element.24.table_ref, bf16[16,108,8,128]{3,2,1,0:T(8,128)(2,1)S(1)} %all_to_all.13.arrived_ref, bf16[16,32,128]{2,1,0:T(8,128)(2,1)S(1)} %get-tuple-element.26.query_ref, ...), custom_call_target="tpu_custom_call" | custom-call | tf_op jit(solution)/shard_map/cond/branch_0_fun/serve/pallas_call | solution.py:242
Async XLA Ops:
  4.5 62.6 %copy-start = (bf16[16,4,1024]{2,1,0:T(4,128)(2,1)S(1)}, bf16[16,4,1024]{2,1,0:T(4,128)(2,1)}, u32[]{:S(2)}) copy-start(bf16[16,4,1024]{2,1,0:T(4,128)(2,1)} %param.14) | copy-start | bytes 393220
  4.5 62.6 %copy-start.1 = (bf16[16,4,256]{2,1,0:T(4,128)(2,1)S(1)}, bf16[16,4,256]{2,1,0:T(4,128)(2,1)}, u32[]{:S(2)}) copy-start(bf16[16,4,256]{2,1,0:T(4,128)(2,1)} %param.15) | copy-start | bytes 98308
  4.6 62.6 %copy-start.2 = (s32[16,8]{0,1:T(8,128)S(1)}, s32[16,8]{0,1:T(8,128)}, u32[]{:S(2)}) copy-start(s32[16,8]{0,1:T(8,128)} %param.13) | copy-start | bytes 1540

commit v4 on v3

--- a/solution.py
+++ b/solution.py
@@ -26,7 +26,7 @@
 SLOTS = GROUPS * REQ_G
 SPAN = MAXP * PAGE
 USUAL = 108
-UNROLL = 8
+UNROLL = 16
 
 VMEM = pl.BlockSpec(memory_space=pltpu.VMEM)
 SMEM = pl.BlockSpec(memory_space=pltpu.SMEM)
@@ -35,71 +35,45 @@
 LIMIT = 40 * 1024 * 1024
 
 
-def cut_kernel(fresh_ref, owner_ref, length_ref, slot_ref, out_ref, pages, owners, facts, ints, sems, table_sem):
-    copies = []
-    for page in range(PAGES_D):
-        copy = pltpu.make_async_copy(fresh_ref.at[page], pages.at[page], sems.at[page])
-        copy.start()
-        copies.append(copy)
-    tables = [
-        pltpu.make_async_copy(owner_ref, owners, table_sem.at[0]),
-        pltpu.make_async_copy(length_ref, facts.at[0], table_sem.at[1]),
-        pltpu.make_async_copy(slot_ref, facts.at[1], table_sem.at[2]),
-    ]
-    for copy in tables:
-        copy.start()
-
-    for page in range(PAGES_D):
-        copies[page].wait()
-        for rt in range(ROW_TILES):
-            for half in range(2):
-                for head in range(KVH):
-                    row = (rt * 2 + half) * KVH + head
-                    out_ref[row, page] = pages[page, head, rt, :, half * HD:(half + 1) * HD]
-
-    for copy in tables:
-        copy.wait()
-    owner = owners[...]
+def cut_kernel(fresh_ref, table_ref, out_ref, ints):
+    owner = table_ref[:MAXP]
     device = (owner * 43) >> 9
     place = device * TILES + (owner - device * PAGES_D)
-    length = facts[0]
+    length = table_ref[MAXP:MAXP + 1]
+    slot = table_ref[MAXP + 1:MAXP + 2]
     ints[...] = jnp.zeros_like(ints)
     for block in range(BLOCKS):
         lanes = slice(block * REQ_G, (block + 1) * REQ_G)
         ints[:ROWS, lanes] = place
         ints[ROWS:ROWS + 1, lanes] = length & (PAGE - 1)
         ints[ROWS + 1:ROWS + 2, lanes] = length >> 6
-        ints[ROWS + 2:ROWS + 3, lanes] = facts[1]
+        ints[ROWS + 2:ROWS + 3, lanes] = slot
     block = lax.broadcasted_iota(jnp.int32, (ROWS, HD), 1) // REQ_G
     mine = lax.rem(lax.axis_index("group"), BLOCKS)
     tile = jnp.where(block == mine, ints[:ROWS], 0)
     tile = jnp.where(block == lax.rem(mine + 1, BLOCKS), ints[ROWS:], tile)
     tile = tile.astype(jnp.float32).astype(jnp.bfloat16)
-    for row in range(GROUPS * TP):
-        out_ref[row, PAGES_D] = tile
+    for rt in range(ROW_TILES):
+        for half in range(2):
+            for head in range(KVH):
+                row = (rt * 2 + half) * KVH + head
+                for page in range(PAGES_D):
+                    out_ref[row, page] = fresh_ref[page, head, rt, :, half * HD:(half + 1) * HD]
+                out_ref[row, PAGES_D] = tile
 
 
 def cut(fresh, owner_table, lengths, decode_slot):
     return pl.pallas_call(
         cut_kernel,
-        in_specs=[HBM, HBM, HBM, HBM],
+        in_specs=[VMEM, VMEM],
         out_specs=VMEM,
         out_shape=jax.ShapeDtypeStruct((GROUPS * TP, TILES, ROWS, HD), jnp.bfloat16),
-        scratch_shapes=[
-            pltpu.VMEM((PAGES_D, KVH, ROW_TILES, ROWS, 2 * HD), jnp.bfloat16),
-            pltpu.VMEM((MAXP, REQ_G), jnp.int32),
-            pltpu.VMEM((2, 1, REQ_G), jnp.int32),
-            pltpu.VMEM((2 * ROWS, HD), jnp.int32),
-            pltpu.SemaphoreType.DMA((PAGES_D,)),
-            pltpu.SemaphoreType.DMA((3,)),
-        ],
-        compiler_params=pltpu.CompilerParams(vmem_limit_bytes=60078000),
+        scratch_shapes=[pltpu.VMEM((2 * ROWS, HD), jnp.int32)],
+        compiler_params=pltpu.CompilerParams(vmem_limit_bytes=LIMIT),
         name="cut",
     )(
         fresh.reshape(PAGES_D, KVH, ROW_TILES, ROWS, 2 * HD),
-        owner_table.T,
-        lengths.reshape(1, REQ_G),
-        decode_slot.reshape(1, REQ_G),
+        jnp.concatenate([owner_table.T, lengths[None], decode_slot[None]], axis=0),
     )
 
 
@@ -131,20 +105,27 @@
     over = jnp.where(first > cap, 1.0, 0.0)
     ints[:ROWS] = sorted_rows[:ROWS] + sorted_rows[10:11] * (TP * TILES)
     ints[ROWS:] = first - count + slot // REQ_G * cap
-    copy = pltpu.make_async_copy(ints, table, sem)
-    copy.start()
+    copies = [
+        pltpu.make_async_copy(ints.at[j], table.at[pl.ds(j * SLOTS, SLOTS)], sem.at[j])
+        for j in range(MAXP + 1)
+    ]
+    for copy in copies:
+        copy.start()
     len_ref[...] = length
     over_ref[0] = jnp.max(over).astype(jnp.int32)
-    copy.wait()
+    for copy in copies:
+        copy.wait()
 
     def fill(group, clamp):
         for item in range(REQ_G):
-            at = table[ROWS, group * REQ_G + item]
+            at = table[group * REQ_G + (ROWS * SLOTS + item)]
+            span = out_ref.at[pl.ds(at, MAXP)]
             for j in reversed(range(MAXP)):
-                place = at + j
+                tile = got_ref[table[group * REQ_G + (j * SLOTS + item)]]
                 if clamp:
-                    place = jnp.minimum(place, GROUPS * cap - 1)
-                out_ref[place] = got_ref[table[j, group * REQ_G + item]]
+                    out_ref[jnp.minimum(at + j, GROUPS * cap - 1)] = tile
+                else:
+                    span[j] = tile
 
     def one_group(group, carry):
         fill(group, False)
@@ -166,8 +147,8 @@
         ],
         scratch_shapes=[
             pltpu.VMEM((2 * ROWS, SLOTS), jnp.int32),
-            pltpu.SMEM((2 * ROWS, SLOTS), jnp.int32),
-            pltpu.SemaphoreType.DMA,
+            pltpu.SMEM(((MAXP + 1) * SLOTS,), jnp.int32),
+            pltpu.SemaphoreType.DMA((MAXP + 1,)),
         ],
         compiler_params=pltpu.CompilerParams(vmem_limit_bytes=LIMIT),
         name="pick",

time: 119 us -> 115 us (0.966)
  Pallas kernels: 14.8 us -> 9.17 us
  local copies, waits for them, and re-layouts: 0.02 us -> 1.91 us
    pallas_call x1, Pallas kernels: 3.9 us -> 0.61 us  [cut(): pl.pallas_call(cut_kernel, in_specs=[VMEM, VMEM], out_specs=VMEM, out_sha...]
    pallas_call x1, Pallas kernels: 6.29 us -> 4.39 us  [pick(): pl.pallas_call(functools.partial(pick_kernel, cap), in_specs=[VMEM], out_...]
    unnamed x6 -> x8, local copies, waits for them, and re-layouts: 0.02 us -> 1.91 us
where the time goes in v4:
time: 115 us
  blocking collectives  102 us (89%)
  Pallas kernels  9.17 us (8%)
  local copies, waits for them, and re-layouts  1.91 us (2%)
  between operations  1.35 us (1%)
    all_to_all x1, blocking collectives, shards(): lax.all_to_all(sent, ('group', 'tp'), split_axis=0, concat_axis=0, tiled=...  55.4 us
    all_to_all x1, blocking collectives, deliver(): lax.all_to_all(packed.reshape(GROUPS, cap, ROWS, HD), 'group', split_axis...  46.6 us
    pallas_call x1, Pallas kernels, pick(): pl.pallas_call(functools.partial(pick_kernel, cap), in_specs=[VMEM], out_...  4.39 us
    pallas_call x1, Pallas kernels, serve(): pl.pallas_call(functools.partial(serve_kernel, arrived.shape[1]), in_spec...  4.16 us

profile of v4, /device:TPU:0, one launch (start us, length us, event | category | flops | bytes accessed | tf_op | source)
XLA Modules:
  0.0 115.1 jit_solution(15125663724001005175)
XLA Ops:
  0.6 0.7 pad_add_fusion.table_ref
  1.4 0.0 copy-start
  1.4 1.9 %copy-done = bf16[12,8,64,256]{3,2,1,0:T(8,128)(2,1)S(1)} copy-done((bf16[12,8,64,256]{3,2,1,0:T(8,128)(2,1)S(1)}, bf16[12,8,64,256]{3,2,1,0:T(8,128)(2,1)}, u32[]{:S(2)}) %copy-start) | copy-done | bytes 3145752
  3.2 0.6 cut.1
  3.9 0.0 copy-start.1
  3.9 0.0 copy-start.2
  3.9 0.0 copy-start.3
  3.9 55.4 %all_to_all.15 = bf16[128,13,8,128]{3,2,1,0:T(8,128)(2,1)S(1)} all-to-all(bf16[128,13,8,128]{3,2,1,0:T(8,128)(2,1)S(1)} %cut.1), channel_id=1, replica_groups=mesh['group'=16,'tp'=8] {'group','tp'}, dimensions={0} | all-to-all | bytes 6815744 | tf_op jit(solution)/shard_map/all_to_all | solution.py:242
  59.3 4.4 %pick.3 = (bf16[1728,8,128]{2,1,0:T(8,128)(2,1)S(1)}, s32[1,256]{1,0:T(1,128)S(1)}, s32[1]{0:T(128)}) custom-call(bf16[1664,8,128]{2,1,0:T(8,128)(2,1)S(1)} %bitcast.22), custom_call_target="tpu_custom_call" | custom-call | tf_op jit(solution)/shard_map/pick/pallas_call | solution.py:139
  64.3 0.0 copy-done.1
  64.3 0.0 copy-done.2
  64.4 0.0 copy-done.3
  64.4 50.7 %conditional.1 = (bf16[16,4,1024]{2,1,0:T(4,128)(2,1)}, bf16[128,1,64,256]{3,2,1,0:T(8,128)(2,1)}) conditional(s32[]{:T(128)} %bitcast.13, (bf16[1728,8,128]{2,1,0:T(8,128)(2,1)S(1)}, s32[1,256]{1,0:T(1,128)S(1)}, s32[8,16]{1,0:T(8,128)S(1)}, bf16[16,32,128]{2,1,0:T(8,128)(2,1)S(1)}, bf16[16,4,256]{2,1,0:T(4,128)(2,1)S(1)}) %tuple.31, ...), branch_computations={%region_0.0_spmd, %region_1.0_spmd} | conditional | bytes 8388624 | solution.py:259
  64.4 46.6 %all_to_all.13.arrived_ref = bf16[16,108,8,128]{3,2,1,0:T(8,128)(2,1)S(1)} all-to-all(bf16[16,108,8,128]{3,2,1,0:T(8,128)(2,1)S(1)} %bitcast.24), channel_id=1, replica_groups=mesh['group'=16,'tp'=8] {'group'}, dimensions={0} | all-to-all | bytes 7077888 | tf_op jit(solution)/shard_map/cond/branch_0_fun/all_to_all | solution.py:249
  110.9 4.2 %serve.2 = (bf16[128,8,8,256]{3,2,1,0:T(8,128)(2,1)}, bf16[16,4,1024]{2,1,0:T(4,128)(2,1)}) custom-call(s32[1,256]{1,0:T(1,128)S(1)} %get-tuple-element.23.len_ref, s32[8,16]{1,0:T(8,128)S(1)} %get-tuple-element.24.table_ref, bf16[16,108,8,128]{3,2,1,0:T(8,128)(2,1)S(1)} %all_to_all.13.arrived_ref, bf16[16,32,128]{2,1,0:T(8,128)(2,1)S(1)} %get-tuple-element.26.query_ref, ...), custom_call_target="tpu_custom_call" | custom-call | tf_op jit(solution)/shard_map/cond/branch_0_fun/serve/pallas_call | solution.py:223
Async XLA Ops:
  1.4 1.9 %copy-start = (bf16[12,8,64,256]{3,2,1,0:T(8,128)(2,1)S(1)}, bf16[12,8,64,256]{3,2,1,0:T(8,128)(2,1)}, u32[]{:S(2)}) copy-start(bf16[12,8,64,256]{3,2,1,0:T(8,128)(2,1)} %param.9) | copy-start | bytes 9437188
  3.9 60.5 %copy-start.1 = (bf16[16,4,1024]{2,1,0:T(4,128)(2,1)S(1)}, bf16[16,4,1024]{2,1,0:T(4,128)(2,1)}, u32[]{:S(2)}) copy-start(bf16[16,4,1024]{2,1,0:T(4,128)(2,1)} %param.14) | copy-start | bytes 393220
  3.9 60.5 %copy-start.2 = (bf16[16,4,256]{2,1,0:T(4,128)(2,1)S(1)}, bf16[16,4,256]{2,1,0:T(4,128)(2,1)}, u32[]{:S(2)}) copy-start(bf16[16,4,256]{2,1,0:T(4,128)(2,1)} %param.15) | copy-start | bytes 98308
  3.9 60.5 %copy-start.3 = (s32[16,8]{0,1:T(8,128)S(1)}, s32[16,8]{0,1:T(8,128)}, u32[]{:S(2)}) copy-start(s32[16,8]{0,1:T(8,128)} %param.13) | copy-start | bytes 1540

commit v5 on v3

--- a/solution.py
+++ b/solution.py
@@ -26,7 +26,7 @@
 SLOTS = GROUPS * REQ_G
 SPAN = MAXP * PAGE
 USUAL = 108
-UNROLL = 8
+UNROLL = 16
 
 VMEM = pl.BlockSpec(memory_space=pltpu.VMEM)
 SMEM = pl.BlockSpec(memory_space=pltpu.SMEM)
@@ -84,7 +84,7 @@
         cut_kernel,
         in_specs=[HBM, HBM, HBM, HBM],
         out_specs=VMEM,
-        out_shape=jax.ShapeDtypeStruct((GROUPS * TP, TILES, ROWS, HD), jnp.bfloat16),
+        out_shape=pltpu.VMEM((GROUPS * TP, TILES, ROWS, HD), jnp.bfloat16),
         scratch_shapes=[
             pltpu.VMEM((PAGES_D, KVH, ROW_TILES, ROWS, 2 * HD), jnp.bfloat16),
             pltpu.VMEM((MAXP, REQ_G), jnp.int32),
@@ -93,7 +93,7 @@
             pltpu.SemaphoreType.DMA((PAGES_D,)),
             pltpu.SemaphoreType.DMA((3,)),
         ],
-        compiler_params=pltpu.CompilerParams(vmem_limit_bytes=60078000),
+        compiler_params=pltpu.CompilerParams(vmem_limit_bytes=58000000),
         name="cut",
     )(
         fresh.reshape(PAGES_D, KVH, ROW_TILES, ROWS, 2 * HD),
@@ -131,20 +131,27 @@
     over = jnp.where(first > cap, 1.0, 0.0)
     ints[:ROWS] = sorted_rows[:ROWS] + sorted_rows[10:11] * (TP * TILES)
     ints[ROWS:] = first - count + slot // REQ_G * cap
-    copy = pltpu.make_async_copy(ints, table, sem)
-    copy.start()
+    copies = [
+        pltpu.make_async_copy(ints.at[j], table.at[pl.ds(j * SLOTS, SLOTS)], sem.at[j])
+        for j in range(MAXP + 1)
+    ]
+    for copy in copies:
+        copy.start()
     len_ref[...] = length
     over_ref[0] = jnp.max(over).astype(jnp.int32)
-    copy.wait()
+    for copy in copies:
+        copy.wait()
 
     def fill(group, clamp):
         for item in range(REQ_G):
-            at = table[ROWS, group * REQ_G + item]
+            at = table[group * REQ_G + (ROWS * SLOTS + item)]
+            span = out_ref.at[pl.ds(at, MAXP)]
             for j in reversed(range(MAXP)):
-                place = at + j
+                tile = got_ref[table[group * REQ_G + (j * SLOTS + item)]]
                 if clamp:
-                    place = jnp.minimum(place, GROUPS * cap - 1)
-                out_ref[place] = got_ref[table[j, group * REQ_G + item]]
+                    out_ref[jnp.minimum(at + j, GROUPS * cap - 1)] = tile
+                else:
+                    span[j] = tile
 
     def one_group(group, carry):
         fill(group, False)
@@ -166,8 +173,8 @@
         ],
         scratch_shapes=[
             pltpu.VMEM((2 * ROWS, SLOTS), jnp.int32),
-            pltpu.SMEM((2 * ROWS, SLOTS), jnp.int32),
-            pltpu.SemaphoreType.DMA,
+            pltpu.SMEM(((MAXP + 1) * SLOTS,), jnp.int32),
+            pltpu.SemaphoreType.DMA((MAXP + 1,)),
         ],
         compiler_params=pltpu.CompilerParams(vmem_limit_bytes=LIMIT),
         name="pick",

time: 119 us -> 114 us (0.958)
  Pallas kernels: 14.8 us -> 10.7 us
    pallas_call x1, Pallas kernels: 6.29 us -> 4.39 us  [pick(): pl.pallas_call(functools.partial(pick_kernel, cap), in_specs=[VMEM], out_...]
    pallas_call x1, Pallas kernels: 3.9 us -> 2.15 us  [cut(): pl.pallas_call(cut_kernel, in_specs=[HBM, HBM, HBM, HBM], out_specs=VMEM,...]
where the time goes in v5:
time: 114 us
  blocking collectives  102 us (89%)
  Pallas kernels  10.7 us (9%)
  between operations  1.34 us (1%)
    all_to_all x1, blocking collectives, shards(): lax.all_to_all(sent, ('group', 'tp'), split_axis=0, concat_axis=0, tiled=...  55.4 us
    all_to_all x1, blocking collectives, deliver(): lax.all_to_all(packed.reshape(GROUPS, cap, ROWS, HD), 'group', split_axis...  46.6 us
    pallas_call x1, Pallas kernels, pick(): pl.pallas_call(functools.partial(pick_kernel, cap), in_specs=[VMEM], out_...  4.39 us
    pallas_call x1, Pallas kernels, serve(): pl.pallas_call(functools.partial(serve_kernel, arrived.shape[1]), in_spec...  4.16 us

profile of v5, /device:TPU:0, one launch (start us, length us, event | category | flops | bytes accessed | tf_op | source)
XLA Modules:
  0.0 114.0 jit_solution(12881783216856400747)
XLA Ops:
  0.6 2.1 %cut.1 = bf16[128,13,8,128]{3,2,1,0:T(8,128)(2,1)S(1)} custom-call(bf16[12,8,8,8,256]{4,3,2,1,0:T(8,128)(2,1)} %bitcast.24, s32[8,16]{1,0:T(8,128)} %bitcast.29, s32[1,16]{1,0:T(1,128)} %bitcast.30, s32[1,16]{1,0:T(1,128)} %bitcast.31), custom_call_target="tpu_custom_call" | custom-call | tf_op jit(solution)/shard_map/cut/pallas_call | solution.py:83
  2.8 0.0 copy-start
  2.8 0.0 copy-start.1
  2.8 0.0 copy-start.2
  2.8 55.4 %all_to_all.15 = bf16[128,13,8,128]{3,2,1,0:T(8,128)(2,1)S(1)} all-to-all(bf16[128,13,8,128]{3,2,1,0:T(8,128)(2,1)S(1)} %cut.1), channel_id=1, replica_groups=mesh['group'=16,'tp'=8] {'group','tp'}, dimensions={0} | all-to-all | bytes 6815744 | tf_op jit(solution)/shard_map/all_to_all | solution.py:268
  58.2 4.4 %pick.3 = (bf16[1728,8,128]{2,1,0:T(8,128)(2,1)S(1)}, s32[1,256]{1,0:T(1,128)S(1)}, s32[1]{0:T(128)}) custom-call(bf16[1664,8,128]{2,1,0:T(8,128)(2,1)S(1)} %bitcast.21), custom_call_target="tpu_custom_call" | custom-call | tf_op jit(solution)/shard_map/pick/pallas_call | solution.py:165
  63.3 0.0 copy-done
  63.3 0.0 copy-done.1
  63.3 0.0 copy-done.2
  63.3 50.7 %conditional.1 = (bf16[16,4,1024]{2,1,0:T(4,128)(2,1)}, bf16[128,1,64,256]{3,2,1,0:T(8,128)(2,1)}) conditional(s32[]{:T(128)} %bitcast.13, (bf16[1728,8,128]{2,1,0:T(8,128)(2,1)S(1)}, s32[1,256]{1,0:T(1,128)S(1)}, s32[8,16]{1,0:T(8,128)S(1)}, bf16[16,32,128]{2,1,0:T(8,128)(2,1)S(1)}, bf16[16,4,256]{2,1,0:T(4,128)(2,1)S(1)}) %tuple.31, ...), branch_computations={%region_0.0_spmd, %region_1.0_spmd} | conditional | bytes 8388624 | solution.py:285
  63.3 46.6 %all_to_all.13.arrived_ref = bf16[16,108,8,128]{3,2,1,0:T(8,128)(2,1)S(1)} all-to-all(bf16[16,108,8,128]{3,2,1,0:T(8,128)(2,1)S(1)} %bitcast.23), channel_id=1, replica_groups=mesh['group'=16,'tp'=8] {'group'}, dimensions={0} | all-to-all | bytes 7077888 | tf_op jit(solution)/shard_map/cond/branch_0_fun/all_to_all | solution.py:275
  109.9 4.2 %serve.2 = (bf16[128,8,8,256]{3,2,1,0:T(8,128)(2,1)}, bf16[16,4,1024]{2,1,0:T(4,128)(2,1)}) custom-call(s32[1,256]{1,0:T(1,128)S(1)} %get-tuple-element.23.len_ref, s32[8,16]{1,0:T(8,128)S(1)} %get-tuple-element.24.table_ref, bf16[16,108,8,128]{3,2,1,0:T(8,128)(2,1)S(1)} %all_to_all.13.arrived_ref, bf16[16,32,128]{2,1,0:T(8,128)(2,1)S(1)} %get-tuple-element.26.query_ref, ...), custom_call_target="tpu_custom_call" | custom-call | tf_op jit(solution)/shard_map/cond/branch_0_fun/serve/pallas_call | solution.py:249
Async XLA Ops:
  2.8 60.5 %copy-start = (bf16[16,4,1024]{2,1,0:T(4,128)(2,1)S(1)}, bf16[16,4,1024]{2,1,0:T(4,128)(2,1)}, u32[]{:S(2)}) copy-start(bf16[16,4,1024]{2,1,0:T(4,128)(2,1)} %param.14) | copy-start | bytes 393220
  2.8 60.5 %copy-start.1 = (bf16[16,4,256]{2,1,0:T(4,128)(2,1)S(1)}, bf16[16,4,256]{2,1,0:T(4,128)(2,1)}, u32[]{:S(2)}) copy-start(bf16[16,4,256]{2,1,0:T(4,128)(2,1)} %param.15) | copy-start | bytes 98308
  2.8 60.5 %copy-start.2 = (s32[16,8]{0,1:T(8,128)S(1)}, s32[16,8]{0,1:T(8,128)}, u32[]{:S(2)}) copy-start(s32[16,8]{0,1:T(8,128)} %param.13) | copy-start | bytes 1540

commit v6 on v5

--- a/solution.py
+++ b/solution.py
@@ -169,7 +169,7 @@
         out_shape=[
             jax.ShapeDtypeStruct((GROUPS * cap, ROWS, HD), jnp.bfloat16),
             jax.ShapeDtypeStruct((1, SLOTS), jnp.int32),
-            jax.ShapeDtypeStruct((1,), jnp.int32),
+            pltpu.SMEM((1,), jnp.int32),
         ],
         scratch_shapes=[
             pltpu.VMEM((2 * ROWS, SLOTS), jnp.int32),
@@ -282,8 +282,8 @@
         return deliver(packed, all_len, ENTRIES)
 
     packed, all_len, over = pick(got, USUAL)
-    pool, attended = lax.cond(
-        over[0] > 0, whole, lambda packed, all_len: deliver(packed, all_len, USUAL), packed, all_len
+    pool, attended = lax.switch(
+        over[0], [lambda packed, all_len: deliver(packed, all_len, USUAL), whole], packed, all_len
     )
     return pool.reshape(ENTRIES, 1, PAGE, 2 * HD), attended
 

time: 114 us -> 113 us (level)
  no operation moved by 1% of the time
where the time goes in v6:
time: 113 us
  blocking collectives  102 us (90%)
  Pallas kernels  10.2 us (9%)
    all_to_all x1, blocking collectives, shards(): lax.all_to_all(sent, ('group', 'tp'), split_axis=0, concat_axis=0, tiled=...  55.4 us
    all_to_all x1, blocking collectives, deliver(): lax.all_to_all(packed.reshape(GROUPS, cap, ROWS, HD), 'group', split_axis...  46.6 us
    pallas_call x1, Pallas kernels, serve(): pl.pallas_call(functools.partial(serve_kernel, arrived.shape[1]), in_spec...  4.16 us
    pallas_call x1, Pallas kernels, pick(): pl.pallas_call(functools.partial(pick_kernel, cap), in_specs=[VMEM], out_...  3.87 us

profile of v6, /device:TPU:0, one launch (start us, length us, event | category | flops | bytes accessed | tf_op | source)
XLA Modules:
  0.0 112.9 jit_solution(7531584677617261263)
XLA Ops:
  0.6 2.1 %cut.1 = bf16[128,13,8,128]{3,2,1,0:T(8,128)(2,1)S(1)} custom-call(bf16[12,8,8,8,256]{4,3,2,1,0:T(8,128)(2,1)} %bitcast.24, s32[8,16]{1,0:T(8,128)} %bitcast.29, s32[1,16]{1,0:T(1,128)} %bitcast.30, s32[1,16]{1,0:T(1,128)} %bitcast.31), custom_call_target="tpu_custom_call" | custom-call | tf_op jit(solution)/shard_map/cut/pallas_call | solution.py:83
  2.8 0.0 copy-start
  2.8 0.0 copy-start.1
  2.8 0.0 copy-start.2
  2.8 55.4 %all_to_all.15 = bf16[128,13,8,128]{3,2,1,0:T(8,128)(2,1)S(1)} all-to-all(bf16[128,13,8,128]{3,2,1,0:T(8,128)(2,1)S(1)} %cut.1), channel_id=1, replica_groups=mesh['group'=16,'tp'=8] {'group','tp'}, dimensions={0} | all-to-all | bytes 6815744 | tf_op jit(solution)/shard_map/all_to_all | solution.py:268
  58.2 3.9 %pick.3 = (bf16[1728,8,128]{2,1,0:T(8,128)(2,1)S(1)}, s32[1,256]{1,0:T(1,128)S(1)}, s32[1]{0:T(128)S(4)}) custom-call(bf16[1664,8,128]{2,1,0:T(8,128)(2,1)S(1)} %bitcast.21), custom_call_target="tpu_custom_call" | custom-call | tf_op jit(solution)/shard_map/pick/pallas_call | solution.py:165
  62.1 0.0 copy-done
  62.1 0.0 copy-done.1
  62.1 0.0 copy-done.2
  62.1 50.7 %conditional.1 = (bf16[16,4,1024]{2,1,0:T(4,128)(2,1)}, bf16[128,1,64,256]{3,2,1,0:T(8,128)(2,1)}) conditional(s32[]{:T(128)} %bitcast.13, (bf16[1728,8,128]{2,1,0:T(8,128)(2,1)S(1)}, s32[1,256]{1,0:T(1,128)S(1)}, s32[8,16]{1,0:T(8,128)S(1)}, bf16[16,32,128]{2,1,0:T(8,128)(2,1)S(1)}, bf16[16,4,256]{2,1,0:T(4,128)(2,1)S(1)}) %tuple.31, ...), branch_computations={%region_0.0_spmd, %region_1.0_spmd} | conditional | bytes 8388624 | solution.py:285
  62.1 46.6 %all_to_all.13.arrived_ref = bf16[16,108,8,128]{3,2,1,0:T(8,128)(2,1)S(1)} all-to-all(bf16[16,108,8,128]{3,2,1,0:T(8,128)(2,1)S(1)} %bitcast.23), channel_id=1, replica_groups=mesh['group'=16,'tp'=8] {'group'}, dimensions={0} | all-to-all | bytes 7077888 | tf_op jit(solution)/shard_map/cond/branch_0_fun/all_to_all | solution.py:275
  108.7 4.2 %serve.2 = (bf16[128,8,8,256]{3,2,1,0:T(8,128)(2,1)}, bf16[16,4,1024]{2,1,0:T(4,128)(2,1)}) custom-call(s32[1,256]{1,0:T(1,128)S(1)} %get-tuple-element.23.len_ref, s32[8,16]{1,0:T(8,128)S(1)} %get-tuple-element.24.table_ref, bf16[16,108,8,128]{3,2,1,0:T(8,128)(2,1)S(1)} %all_to_all.13.arrived_ref, bf16[16,32,128]{2,1,0:T(8,128)(2,1)S(1)} %get-tuple-element.26.query_ref, ...), custom_call_target="tpu_custom_call" | custom-call | tf_op jit(solution)/shard_map/cond/branch_0_fun/serve/pallas_call | solution.py:249
Async XLA Ops:
  2.8 59.3 %copy-start = (bf16[16,4,1024]{2,1,0:T(4,128)(2,1)S(1)}, bf16[16,4,1024]{2,1,0:T(4,128)(2,1)}, u32[]{:S(2)}) copy-start(bf16[16,4,1024]{2,1,0:T(4,128)(2,1)} %param.14) | copy-start | bytes 393220
  2.8 59.3 %copy-start.1 = (bf16[16,4,256]{2,1,0:T(4,128)(2,1)S(1)}, bf16[16,4,256]{2,1,0:T(4,128)(2,1)}, u32[]{:S(2)}) copy-start(bf16[16,4,256]{2,1,0:T(4,128)(2,1)} %param.15) | copy-start | bytes 98308
  2.8 59.3 %copy-start.2 = (s32[16,8]{0,1:T(8,128)S(1)}, s32[16,8]{0,1:T(8,128)}, u32[]{:S(2)}) copy-start(s32[16,8]{0,1:T(8,128)} %param.13) | copy-start | bytes 1540
